TPU v7x, 128 devices: a whole 4x4x4 slice. The times are simulated.
128 devices in a mesh: grp: 4 (over x), sta: 32 (over z, y, core).
Axes of the slice: x: 4, y: 4, z: 4, core: 2. Of those that a mesh axis runs over, the one named last changes fastest.
Arguments:
- spectra: float32 [1024, 2, 18432], P(('grp', 'sta')), may hold values from -61 to 61
- stacks: float32 [12288, 1601], P(('grp', 'sta')), may hold values from -6 to 6
- pair_sta: int32 [2, 12288], P(None, ('grp', 'sta')), may hold values from 0 to 255
- pair_valid: int32 [12288], P(('grp', 'sta')), may hold values 0 or 1
- owner: int32 [12288, 1], P(('grp', 'sta')), may hold values from 0 to 127; in each aligned block of 96 rows (0 to 95, 96 to 191, ...) at most 2 rows name the same one
- slot: int32 [12288], P(('grp', 'sta')), may hold values from 0 to 95
Outputs:
- stacks_new: float32 [12288, 1601], P(('grp', 'sta'))
Inputs may be any that keep to these rules, and one draw needn't show every extreme that they name: Among the 96 rows of one device no owner is named more than 2 times.
All inputs are finite; a program needn't handle non-finite values. No bound on the sum of `pair_valid` on one device may be relied on, other than what follows from the above.
Results may differ from a plain program's by a relative error of at most 0.0041.
Values may be sent and summed in bfloat16 or wider, within the bound.
A program may use at most 128 MiB of HBM per device.

v0:
```python
import math

import jax
import jax.numpy as jnp
from jax import lax
from jax.sharding import PartitionSpec as P

BAND = 64


def cut_along(x, dim, length):
    shape = x.shape
    tiles = x.reshape(*shape[:dim], length, shape[dim] // length, *shape[dim + 1 :])
    return jnp.moveaxis(tiles, dim, 0)


def joined_along(tiles, dim):
    shape = list(tiles.shape[1:])
    shape[dim] *= tiles.shape[0]
    return jnp.moveaxis(tiles, 0, dim).reshape(shape)


def joined_exchange(x, axis, axes, splits, concats):
    sizes = [lax.axis_size(a) for a in axes]
    tiles = cut_along(x, splits[0], sizes[0])
    tiles = jnp.moveaxis(cut_along(tiles, splits[1] + 1, sizes[1]), 0, 1)
    inside = tiles.shape[2:]
    tiles = tiles.reshape(-1, *inside)
    tiles = lax.all_to_all(tiles, axis, split_axis=0, concat_axis=0, tiled=True)
    tiles = joined_along(tiles.reshape(*sizes, *inside), concats[0] + 1)
    return joined_along(tiles, concats[1])


def whiten(spectra):
    shape = spectra.shape
    split = spectra.reshape(shape[0], 2, shape[2] // BAND, BAND)
    power = jnp.mean(split * split, axis=(1, 3), keepdims=True)
    return (split * lax.rsqrt(power + 1e-06)).reshape(shape).astype(jnp.bfloat16)


def table_block(start, width, lag_count, total_bins):
    freqs = start + lax.iota(jnp.int32, width)
    shifts = lax.iota(jnp.int32, lag_count) - (lag_count - 1) // 2
    angle_ids = jnp.mod(freqs[:, None] * shifts[None, :], 2 * total_bins)
    theta = angle_ids.astype(jnp.float32) * jnp.float32(math.pi / total_bins)
    return (jnp.cos(theta).astype(jnp.bfloat16), (-jnp.sin(theta)).astype(jnp.bfloat16))


def local(spectra, stacks, pair_sta, pair_valid, owner, slot):
    total_bins = spectra.shape[2]
    lag_count = stacks.shape[1]
    stack_rows = stacks.shape[0]
    pair_count = pair_sta.shape[1]
    groups = lax.axis_size("grp")
    members = lax.axis_size("sta")
    devices = groups * members
    capacity = max(2, (4 * pair_count + 3 * devices - 1) // (3 * devices))
    whitened = whiten(spectra)
    gathered = lax.all_gather(whitened, "sta", axis=0, tiled=True)
    first = jnp.take(gathered, pair_sta[0], axis=0)
    second = jnp.take(gathered, pair_sta[1], axis=0)
    fblock = 2048

    def add_block(index, total):
        start = index * fblock
        left = lax.dynamic_slice_in_dim(first, start, fblock, 2).astype(jnp.float32)
        right = lax.dynamic_slice_in_dim(second, start, fblock, 2).astype(jnp.float32)
        real_part = (left[:, 0] * right[:, 0] + left[:, 1] * right[:, 1]).astype(jnp.bfloat16)
        imag_part = (left[:, 1] * right[:, 0] - left[:, 0] * right[:, 1]).astype(jnp.bfloat16)
        cosines, sines = table_block(start, fblock, lag_count, total_bins)
        total = total + jnp.dot(real_part, cosines, preferred_element_type=jnp.float32)
        return total + jnp.dot(imag_part, sines, preferred_element_type=jnp.float32)

    corr = lax.fori_loop(
        0, total_bins // fblock, add_block, jnp.zeros((pair_count, lag_count), jnp.float32)
    )
    corr = corr * jnp.float32(total_bins ** (-0.5)) * pair_valid.astype(jnp.float32)[:, None]
    dest = owner[:, 0]
    dest_hot = (dest[:, None] == lax.iota(jnp.int32, devices)[None, :]).astype(jnp.int32)
    before = jnp.cumsum(dest_hot, axis=0) - dest_hot
    position = jnp.sum(before * dest_hot, axis=1)
    flat = dest * capacity + position
    placing = (flat[:, None] == lax.iota(jnp.int32, devices * capacity)[None, :]).astype(
        jnp.float32
    )
    send_rows = jnp.dot(placing.T, corr, precision=lax.Precision.HIGHEST)
    send_slots = jnp.dot(
        placing.T, slot.astype(jnp.float32)[:, None], precision=lax.Precision.HIGHEST
    )[:, 0]
    got_rows, got_slots = (
        joined_exchange(
            send_rows.reshape(groups, members, capacity, lag_count),
            ("grp", "sta"),
            ("grp", "sta"),
            (0, 1),
            (0, 1),
        ),
        joined_exchange(
            send_slots.reshape(groups, members, capacity),
            ("grp", "sta"),
            ("grp", "sta"),
            (0, 1),
            (0, 1),
        ),
    )
    got_rows = got_rows.reshape(devices * capacity, lag_count)
    got_slots = got_slots.reshape(devices * capacity)
    adding = (
        got_slots[None, :] == lax.iota(jnp.int32, stack_rows).astype(jnp.float32)[:, None]
    ).astype(jnp.float32)
    return stacks + jnp.dot(adding, got_rows, precision=lax.Precision.HIGHEST)


def solution(mesh):
    return jax.shard_map(
        local,
        mesh=mesh,
        in_specs=(
            P(("grp", "sta"), None, None),
            P(("grp", "sta"), None),
            P(None, ("grp", "sta")),
            P(("grp", "sta")),
            P(("grp", "sta"), None),
            P(("grp", "sta")),
        ),
        out_specs=P(("grp", "sta"), None),
        check_vma=False,
    )
```

profile of v0, /device:TPU:1, one launch (start us, length us, event | category | flops | bytes accessed | tf_op | source)
XLA Modules:
  0.0 1220.7 jit_solution(18075538447004292541)
XLA Ops:
  6.6 2.9 multiply_reduce_fusion
  14.1 11.5 all-to-all-start
  25.7 68.5 %all-gather.2.cloned.1.call-done = bf16[256,2,18432]{2,1,0:T(2,128)(2,1)} async-done(((bf16[8,2,18432]{2,1,0:T(2,128)(2,1)}), bf16[256,2,18432]{2,1,0:T(2,128)(2,1)}) %all-gather.2.cloned.1.call-update) | async-done | bytes 18874384 | tf_op jit(solution)/shard_map/all_gather | solution.py:59
  94.3 23.4 %gather_fusion = bf16[96,2,18432]{2,1,0:T(2,128)(2,1)} fusion(bf16[256,2,18432]{2,1,0:T(2,128)(2,1)} %all-gather.2.cloned.1.call-done, s32[1024]{0:T(1024)S(1)} %pad_clamp_fusion.1), kind=kCustom, calls=%fused_computation.clone | custom fusion | bytes 14156160 | tf_op jit(solution)/shard_map/jit(_take)/gather | solution.py:60
  117.6 23.3 %gather_fusion.1 = bf16[96,2,18432]{2,1,0:T(2,128)(2,1)} fusion(bf16[256,2,18432]{2,1,0:T(2,128)(2,1)} %all-gather.2.cloned.1.call-done, s32[1024]{0:T(1024)S(1)} %pad_clamp_fusion), kind=kCustom, calls=%fused_computation.1.clone | custom fusion | bytes 14156160 | tf_op jit(solution)/shard_map/jit(_take)/gather | solution.py:61
  140.9 16.3 %broadcast_select_fusion = (bf16[96,2,18432]{2,1,0:T(2,128)(2,1)}, bf16[96,2,18432]{2,1,0:T(2,128)(2,1)}) fusion(bf16[96,2,18432]{2,1,0:T(2,128)(2,1)} %gather_fusion.1, pred[96]{0:T(512)(128)(4,1)S(1)} %get-tuple-element.150, bf16[96,2,18432]{2,1,0:T(2,128)(2,1)} %gather_fusion, pred[96]{0:T(512)(128)(4,1)S(1)} %get-tuple-element.156), kind=kLoop, calls=%fused_computation.31 | loop fusion | flops 7077888 | bytes 28311744 | tf_op jit(solution)/shard_map/jit(_take)/select_n | solution.py:61
  157.2 1014.8 %while.16 = (s32[]{:T(128)}, f32[96,1601]{1,0:T(8,128)}, bf16[96,2,18432]{2,1,0:T(2,128)(2,1)}, bf16[96,2,18432]{2,1,0:T(2,128)(2,1)}, s32[]{:T(128)}, /*index=5*/s32[]{:T(128)}, s32[]{:T(128)}, s32[]{:T(128)}) while((s32[]{:T(128)}, f32[96,1601]{1,0:T(8,128)}, bf16[96,2,18432]{2,1,0:T(2,128)(2,1)}, ...), condition=%wide.region_5.7_spmd.clone, body=%wide.region_4.6_spmd.clone.sunk | while | flops 1330757632 | bytes 16658849 | solution.py:74
  177.0 2.5 constant_dynamic-slice_fusion.3
  180.0 52.4 %fusion.42 = f32[96,1601]{1,0:T(8,128)S(1)} fusion(s32[1601]{0:T(1024)S(1)} %iota_add_fusion.4, s32[2048]{0:T(1024)S(1)} %iota_add_fusion.5, f32[96,1601]{1,0:T(8,128)} %get-tuple-element.198, f32[96,2,2048]{2,0,1:T(8,128)S(1)} %copy_convert_fusion.4, f32[96,2,2048]{2,0,1:T(8,128)S(1)} %copy_convert_fusion.5, pred[]{:T(512)S(6)} %compare.3), kind=kOutput, calls=%fused_computation.14.clone.3 | convolution fusion | flops 663421184 | bytes 4389893 | tf_op jit(solution)/shard_map/while/body/eval_jaxpr/dot_general | solution.py:71
  232.5 54.1 %fusion.43 = f32[96,1601]{1,0:T(8,128)} fusion(f32[96,1601]{1,0:T(8,128)S(1)} %fusion.42, s32[1601]{0:T(1024)S(1)} %iota_add_fusion.4, s32[2048]{0:T(1024)S(1)} %iota_add_fusion.5, f32[96,2,2048]{2,0,1:T(8,128)S(1)} %copy_convert_fusion.4, f32[96,2,2048]{2,0,1:T(8,128)S(1)} %copy_convert_fusion.5), kind=kOutput, calls=%fused_computation.13.clone.3 | convolution fusion | flops 666546304 | bytes 4389892 | tf_op jit(solution)/shard_map/while/body/eval_jaxpr/dot_general | solution.py:72
  286.6 2.5 constant_dynamic-slice_fusion.3
  289.6 53.5 %fusion.42 = f32[96,1601]{1,0:T(8,128)S(1)} fusion(s32[1601]{0:T(1024)S(1)} %iota_add_fusion.4, s32[2048]{0:T(1024)S(1)} %iota_add_fusion.5, f32[96,1601]{1,0:T(8,128)} %get-tuple-element.198, f32[96,2,2048]{2,0,1:T(8,128)S(1)} %copy_convert_fusion.4, f32[96,2,2048]{2,0,1:T(8,128)S(1)} %copy_convert_fusion.5, pred[]{:T(512)S(6)} %compare.3), kind=kOutput, calls=%fused_computation.14.clone.3 | convolution fusion | flops 663421184 | bytes 4389893 | tf_op jit(solution)/shard_map/while/body/eval_jaxpr/dot_general | solution.py:71
  343.1 54.1 %fusion.43 = f32[96,1601]{1,0:T(8,128)} fusion(f32[96,1601]{1,0:T(8,128)S(1)} %fusion.42, s32[1601]{0:T(1024)S(1)} %iota_add_fusion.4, s32[2048]{0:T(1024)S(1)} %iota_add_fusion.5, f32[96,2,2048]{2,0,1:T(8,128)S(1)} %copy_convert_fusion.4, f32[96,2,2048]{2,0,1:T(8,128)S(1)} %copy_convert_fusion.5), kind=kOutput, calls=%fused_computation.13.clone.3 | convolution fusion | flops 666546304 | bytes 4389892 | tf_op jit(solution)/shard_map/while/body/eval_jaxpr/dot_general | solution.py:72
  400.2 53.5 %fusion.42 = f32[96,1601]{1,0:T(8,128)S(1)} fusion(s32[1601]{0:T(1024)S(1)} %iota_add_fusion.4, s32[2048]{0:T(1024)S(1)} %iota_add_fusion.5, f32[96,1601]{1,0:T(8,128)} %get-tuple-element.198, f32[96,2,2048]{2,0,1:T(8,128)S(1)} %copy_convert_fusion.4, f32[96,2,2048]{2,0,1:T(8,128)S(1)} %copy_convert_fusion.5, pred[]{:T(512)S(6)} %compare.3), kind=kOutput, calls=%fused_computation.14.clone.3 | convolution fusion | flops 663421184 | bytes 4389893 | tf_op jit(solution)/shard_map/while/body/eval_jaxpr/dot_general | solution.py:71
  453.8 54.1 %fusion.43 = f32[96,1601]{1,0:T(8,128)} fusion(f32[96,1601]{1,0:T(8,128)S(1)} %fusion.42, s32[1601]{0:T(1024)S(1)} %iota_add_fusion.4, s32[2048]{0:T(1024)S(1)} %iota_add_fusion.5, f32[96,2,2048]{2,0,1:T(8,128)S(1)} %copy_convert_fusion.4, f32[96,2,2048]{2,0,1:T(8,128)S(1)} %copy_convert_fusion.5), kind=kOutput, calls=%fused_computation.13.clone.3 | convolution fusion | flops 666546304 | bytes 4389892 | tf_op jit(solution)/shard_map/while/body/eval_jaxpr/dot_general | solution.py:72
  507.9 2.5 constant_dynamic-slice_fusion.3
  510.9 53.5 %fusion.42 = f32[96,1601]{1,0:T(8,128)S(1)} fusion(s32[1601]{0:T(1024)S(1)} %iota_add_fusion.4, s32[2048]{0:T(1024)S(1)} %iota_add_fusion.5, f32[96,1601]{1,0:T(8,128)} %get-tuple-element.198, f32[96,2,2048]{2,0,1:T(8,128)S(1)} %copy_convert_fusion.4, f32[96,2,2048]{2,0,1:T(8,128)S(1)} %copy_convert_fusion.5, pred[]{:T(512)S(6)} %compare.3), kind=kOutput, calls=%fused_computation.14.clone.3 | convolution fusion | flops 663421184 | bytes 4389893 | tf_op jit(solution)/shard_map/while/body/eval_jaxpr/dot_general | solution.py:71
  564.4 54.1 %fusion.43 = f32[96,1601]{1,0:T(8,128)} fusion(f32[96,1601]{1,0:T(8,128)S(1)} %fusion.42, s32[1601]{0:T(1024)S(1)} %iota_add_fusion.4, s32[2048]{0:T(1024)S(1)} %iota_add_fusion.5, f32[96,2,2048]{2,0,1:T(8,128)S(1)} %copy_convert_fusion.4, f32[96,2,2048]{2,0,1:T(8,128)S(1)} %copy_convert_fusion.5), kind=kOutput, calls=%fused_computation.13.clone.3 | convolution fusion | flops 666546304 | bytes 4389892 | tf_op jit(solution)/shard_map/while/body/eval_jaxpr/dot_general | solution.py:72
  618.5 2.5 constant_dynamic-slice_fusion.3
  621.5 53.5 %fusion.42 = f32[96,1601]{1,0:T(8,128)S(1)} fusion(s32[1601]{0:T(1024)S(1)} %iota_add_fusion.4, s32[2048]{0:T(1024)S(1)} %iota_add_fusion.5, f32[96,1601]{1,0:T(8,128)} %get-tuple-element.198, f32[96,2,2048]{2,0,1:T(8,128)S(1)} %copy_convert_fusion.4, f32[96,2,2048]{2,0,1:T(8,128)S(1)} %copy_convert_fusion.5, pred[]{:T(512)S(6)} %compare.3), kind=kOutput, calls=%fused_computation.14.clone.3 | convolution fusion | flops 663421184 | bytes 4389893 | tf_op jit(solution)/shard_map/while/body/eval_jaxpr/dot_general | solution.py:71
  675.1 54.1 %fusion.43 = f32[96,1601]{1,0:T(8,128)} fusion(f32[96,1601]{1,0:T(8,128)S(1)} %fusion.42, s32[1601]{0:T(1024)S(1)} %iota_add_fusion.4, s32[2048]{0:T(1024)S(1)} %iota_add_fusion.5, f32[96,2,2048]{2,0,1:T(8,128)S(1)} %copy_convert_fusion.4, f32[96,2,2048]{2,0,1:T(8,128)S(1)} %copy_convert_fusion.5), kind=kOutput, calls=%fused_computation.13.clone.3 | convolution fusion | flops 666546304 | bytes 4389892 | tf_op jit(solution)/shard_map/while/body/eval_jaxpr/dot_general | solution.py:72
  732.2 53.5 %fusion.42 = f32[96,1601]{1,0:T(8,128)S(1)} fusion(s32[1601]{0:T(1024)S(1)} %iota_add_fusion.4, s32[2048]{0:T(1024)S(1)} %iota_add_fusion.5, f32[96,1601]{1,0:T(8,128)} %get-tuple-element.198, f32[96,2,2048]{2,0,1:T(8,128)S(1)} %copy_convert_fusion.4, f32[96,2,2048]{2,0,1:T(8,128)S(1)} %copy_convert_fusion.5, pred[]{:T(512)S(6)} %compare.3), kind=kOutput, calls=%fused_computation.14.clone.3 | convolution fusion | flops 663421184 | bytes 4389893 | tf_op jit(solution)/shard_map/while/body/eval_jaxpr/dot_general | solution.py:71
  785.7 54.1 %fusion.43 = f32[96,1601]{1,0:T(8,128)} fusion(f32[96,1601]{1,0:T(8,128)S(1)} %fusion.42, s32[1601]{0:T(1024)S(1)} %iota_add_fusion.4, s32[2048]{0:T(1024)S(1)} %iota_add_fusion.5, f32[96,2,2048]{2,0,1:T(8,128)S(1)} %copy_convert_fusion.4, f32[96,2,2048]{2,0,1:T(8,128)S(1)} %copy_convert_fusion.5), kind=kOutput, calls=%fused_computation.13.clone.3 | convolution fusion | flops 666546304 | bytes 4389892 | tf_op jit(solution)/shard_map/while/body/eval_jaxpr/dot_general | solution.py:72
  842.9 53.5 %fusion.42 = f32[96,1601]{1,0:T(8,128)S(1)} fusion(s32[1601]{0:T(1024)S(1)} %iota_add_fusion.4, s32[2048]{0:T(1024)S(1)} %iota_add_fusion.5, f32[96,1601]{1,0:T(8,128)} %get-tuple-element.198, f32[96,2,2048]{2,0,1:T(8,128)S(1)} %copy_convert_fusion.4, f32[96,2,2048]{2,0,1:T(8,128)S(1)} %copy_convert_fusion.5, pred[]{:T(512)S(6)} %compare.3), kind=kOutput, calls=%fused_computation.14.clone.3 | convolution fusion | flops 663421184 | bytes 4389893 | tf_op jit(solution)/shard_map/while/body/eval_jaxpr/dot_general | solution.py:71
  896.4 54.1 %fusion.43 = f32[96,1601]{1,0:T(8,128)} fusion(f32[96,1601]{1,0:T(8,128)S(1)} %fusion.42, s32[1601]{0:T(1024)S(1)} %iota_add_fusion.4, s32[2048]{0:T(1024)S(1)} %iota_add_fusion.5, f32[96,2,2048]{2,0,1:T(8,128)S(1)} %copy_convert_fusion.4, f32[96,2,2048]{2,0,1:T(8,128)S(1)} %copy_convert_fusion.5), kind=kOutput, calls=%fused_computation.13.clone.3 | convolution fusion | flops 666546304 | bytes 4389892 | tf_op jit(solution)/shard_map/while/body/eval_jaxpr/dot_general | solution.py:72
  953.5 53.5 %fusion.42 = f32[96,1601]{1,0:T(8,128)S(1)} fusion(s32[1601]{0:T(1024)S(1)} %iota_add_fusion.4, s32[2048]{0:T(1024)S(1)} %iota_add_fusion.5, f32[96,1601]{1,0:T(8,128)} %get-tuple-element.198, f32[96,2,2048]{2,0,1:T(8,128)S(1)} %copy_convert_fusion.4, f32[96,2,2048]{2,0,1:T(8,128)S(1)} %copy_convert_fusion.5, pred[]{:T(512)S(6)} %compare.3), kind=kOutput, calls=%fused_computation.14.clone.3 | convolution fusion | flops 663421184 | bytes 4389893 | tf_op jit(solution)/shard_map/while/body/eval_jaxpr/dot_general | solution.py:71
  1007.0 54.1 %fusion.43 = f32[96,1601]{1,0:T(8,128)} fusion(f32[96,1601]{1,0:T(8,128)S(1)} %fusion.42, s32[1601]{0:T(1024)S(1)} %iota_add_fusion.4, s32[2048]{0:T(1024)S(1)} %iota_add_fusion.5, f32[96,2,2048]{2,0,1:T(8,128)S(1)} %copy_convert_fusion.4, f32[96,2,2048]{2,0,1:T(8,128)S(1)} %copy_convert_fusion.5), kind=kOutput, calls=%fused_computation.13.clone.3 | convolution fusion | flops 666546304 | bytes 4389892 | tf_op jit(solution)/shard_map/while/body/eval_jaxpr/dot_general | solution.py:72
  1064.2 53.5 %fusion.42 = f32[96,1601]{1,0:T(8,128)S(1)} fusion(s32[1601]{0:T(1024)S(1)} %iota_add_fusion.4, s32[2048]{0:T(1024)S(1)} %iota_add_fusion.5, f32[96,1601]{1,0:T(8,128)} %get-tuple-element.198, f32[96,2,2048]{2,0,1:T(8,128)S(1)} %copy_convert_fusion.4, f32[96,2,2048]{2,0,1:T(8,128)S(1)} %copy_convert_fusion.5, pred[]{:T(512)S(6)} %compare.3), kind=kOutput, calls=%fused_computation.14.clone.3 | convolution fusion | flops 663421184 | bytes 4389893 | tf_op jit(solution)/shard_map/while/body/eval_jaxpr/dot_general | solution.py:71
  1117.7 54.1 %fusion.43 = f32[96,1601]{1,0:T(8,128)} fusion(f32[96,1601]{1,0:T(8,128)S(1)} %fusion.42, s32[1601]{0:T(1024)S(1)} %iota_add_fusion.4, s32[2048]{0:T(1024)S(1)} %iota_add_fusion.5, f32[96,2,2048]{2,0,1:T(8,128)S(1)} %copy_convert_fusion.4, f32[96,2,2048]{2,0,1:T(8,128)S(1)} %copy_convert_fusion.5), kind=kOutput, calls=%fused_computation.13.clone.3 | convolution fusion | flops 666546304 | bytes 4389892 | tf_op jit(solution)/shard_map/while/body/eval_jaxpr/dot_general | solution.py:72
  1176.2 7.2 all-to-all-start.1
  1183.6 26.0 %all-to-all-done.1 = f32[128,1,1,2,1601]{4,3,2,1,0:T(2,128)S(1)} async-done(((f32[128,1,1,2,1601]{4,3,2,1,0:T(2,128)}), f32[128,1,1,2,1601]{4,3,2,1,0:T(2,128)S(1)}, u32[]{:S(2)}, u32[]{:S(2)}) %all-to-all-start.1) | async-done | bytes 1639456 | tf_op jit(solution)/shard_map/all_to_all | solution.py:29
  1210.8 2.7 convolution_add_fusion
  (77 shorter events, 27.3 us)
Async XLA Ops:
  6.5 4.7 copy-start
  6.5 6.2 copy-start.3
  6.5 6.2 copy-start.1
  6.5 19.1 %copy-start.2 = (s32[2,96]{1,0:T(2,128)S(1)}, s32[2,96]{1,0:T(2,128)}, u32[]{:S(2)}) copy-start(s32[2,96]{1,0:T(2,128)} %param.12) | copy-start | bytes 2308
  6.5 19.2 %copy-start.4 = (s32[96]{0:T(128)S(1)}, s32[96]{0:T(128)}, u32[]{:S(2)}) copy-start(s32[96]{0:T(128)} %param.13) | copy-start | bytes 1156
  6.5 87.7 %all-gather.2.cloned.1.call-start = ((), (), s32[]{:S(2)}) async-start(), calls=%async_computation.2 | async-start | bytes 19464192 | tf_op jit(solution)/shard_map/all_gather | solution.py:59
  14.1 1162.1 %all-to-all-start = ((f32[128,1,1,2]{3,2,1,0:T(1,128)}), f32[128,1,1,2]{3,2,1,0:T(1,128)S(1)}, u32[]{:S(2)}, u32[]{:S(2)}) async-start(f32[128,1,1,2]{3,2,1,0:T(1,128)} %bitcast.4), calls=%async_computation | async-start | bytes 131072 | tf_op jit(solution)/shard_map/all_to_all | solution.py:29
  1176.2 33.4 %all-to-all-start.1 = ((f32[128,1,1,2,1601]{4,3,2,1,0:T(2,128)}), f32[128,1,1,2,1601]{4,3,2,1,0:T(2,128)S(1)}, u32[]{:S(2)}, u32[]{:S(2)}) async-start(f32[128,1,1,2,1601]{4,3,2,1,0:T(2,128)} %bitcast.11), calls=%async_computation.1 | async-start | bytes 3407872 | tf_op jit(solution)/shard_map/all_to_all | solution.py:29
Sparse Core Ops, SparseCore 0:
  12.8 81.4 all-gather.1
where the time goes:
time: 1230 us; the launch traced here: 1220 us
  matrix products  972 us (79%)
  waiting for transfers between devices  94.5 us (8%)
  local copies, waits for them, and re-layouts  73.5 us (6%)
  other arithmetic  27.4 us (2%)
  loops' own time  20.3 us (2%)
  starting transfers between devices  18.8 us (2%)
  between operations  14 us (1%)
    dot_general x9, matrix products, add_block(): return total + jnp.dot(imag_part, sines, preferred_element_type=jnp.float32)  487 us
    dot_general x9, matrix products, add_block(): jnp.dot(real_part, cosines, preferred_element_type=jnp.float32)  481 us
    all_gather x1, waiting for transfers between devices, local(): gathered = lax.all_gather(whitened, 'sta', axis=0, tiled=True)  68.5 us
    all_to_all x2, waiting for transfers between devices, joined_exchange(): tiles = lax.all_to_all(tiles, axis, split_axis=0, concat_axis=0, tiled=True)  26 us
  transfers between devices with their start and end apart: 3, of which 2 were waited for; matrix products, arithmetic and copies ran while one was open for 87% of the time, Pallas kernels for 0%

commit v1 on v0

v1 whole, which is shorter than its diff:
```python
import functools
import math

import jax
import jax.numpy as jnp
from jax import lax
from jax.experimental import pallas as pl
from jax.experimental.pallas import tpu as pltpu
from jax.sharding import PartitionSpec as P

BAND = 64
MESH = pl.DeviceIdType.MESH
BF16 = jnp.bfloat16
F32 = jnp.float32

BINS = 18432
LAGS = 1601
LAGP = 1664
PAIRS = 96
RING = 8
SLAB = BINS // RING
CHUNKS = 6
CW = SLAB // CHUNKS
MEMBERS = 32
GROUPS = 4
DEVS = 128
STATIONS = 256
SEG = 256
SEGS = 7


def angles(freqs, shifts):
    product = (freqs * shifts).astype(F32)
    turns = jnp.floor(product * F32(1.0 / (2 * BINS)))
    return (product - turns * F32(2 * BINS)) * F32(math.pi / BINS)


def main_kernel(
    x_ref, ids_ref, code_ref, slot_ref, got_ref,
    ws, wr, wc, ids_all, sel, table, acc, cross, a_send, a_recv, b_send, b_recv,
    corr2, gsel, c_send,
    id_send_sem, id_recv_sem, w_send_sem, w_recv_sem,
    a_send_sem, a_recv_sem, b_send_sem, b_recv_sem, c_send_sem, c_recv_sem, own_sem,
):
    grp = lax.axis_index("grp")
    me = lax.axis_index("sta")
    dev = grp * MEMBERS + me
    my_slab = lax.rem(me, RING)
    row = me - my_slab
    my_y = my_slab // 2
    my_c = lax.rem(my_slab, 2)

    barrier = pltpu.get_barrier_semaphore()

    def greet(i, carry):
        peer = lax.rem(dev + i, DEVS)
        pl.semaphore_signal(
            barrier, inc=1,
            device_id={"grp": peer // MEMBERS, "sta": lax.rem(peer, MEMBERS)},
            device_id_type=MESH,
        )
        return carry

    lax.fori_loop(1, DEVS, greet, 0)

    lane = lax.broadcasted_iota(jnp.int32, (128, 128), 1) // BAND
    sub = lax.broadcasted_iota(jnp.int32, (128, 128), 0) // BAND
    bands = jnp.where(lane == sub, F32(1), F32(0))

    def whiten(s, carry):
        base = pl.multiple_of(s * SLAB, 128)
        x0 = x_ref[0, :, pl.ds(base, SLAB)]
        x1 = x_ref[1, :, pl.ds(base, SLAB)]
        square = x0 * x0 + x1 * x1
        tiles = SLAB // 128
        rows = jnp.concatenate([square[:, j * 128 : (j + 1) * 128] for j in range(tiles)], axis=0)
        power = jnp.dot(
            rows, bands, precision=lax.Precision.HIGHEST, preferred_element_type=F32
        ) * F32(1.0 / (2 * BAND))
        inverse = lax.rsqrt(power + F32(1e-06))
        for j in range(tiles):
            inv = inverse[j * 8 : (j + 1) * 8]
            cut = slice(j * 128, (j + 1) * 128)
            both = jnp.concatenate([x0[:, cut] * inv, x1[:, cut] * inv], axis=0).astype(BF16)
            q, o = divmod(j, CW // 128)
            ws[s, q, :, o * 128 : (o + 1) * 128] = both
        return carry

    lax.fori_loop(0, RING, whiten, 0)
    pl.semaphore_wait(barrier, DEVS - 1)

    def send_ids(i, carry):
        peer = row + lax.rem(my_slab + i, RING)
        pltpu.make_async_remote_copy(
            src_ref=ids_ref, dst_ref=ids_all.at[my_slab],
            send_sem=id_send_sem, recv_sem=id_recv_sem,
            device_id={"sta": peer}, device_id_type=MESH,
        ).start()
        return carry

    lax.fori_loop(1, RING, send_ids, 0)
    ids_all[my_slab] = ids_ref[...]

    def send_chunk(q, carry):
        def one(i, inner):
            peer = lax.rem(me + i, MEMBERS)
            pltpu.make_async_remote_copy(
                src_ref=ws.at[lax.rem(peer, RING), q], dst_ref=wr.at[q, me],
                send_sem=w_send_sem.at[q], recv_sem=w_recv_sem.at[q],
                device_id={"sta": peer}, device_id_type=MESH,
            ).start()
            return inner

        lax.fori_loop(1, MEMBERS, one, 0)
        wr[q, me] = ws[my_slab, q]
        return carry

    lax.fori_loop(0, CHUNKS, send_chunk, 0)

    start = my_slab * SLAB

    def table_column(cb, carry):
        lags = lax.broadcasted_iota(jnp.int32, (64, 128), 1) + (cb * 128 - (LAGS - 1) // 2)
        freqs = lax.broadcasted_iota(jnp.int32, (64, 128), 0) + start
        theta = angles(freqs, lags)
        cosines, sines = jnp.cos(theta), jnp.sin(theta)
        turn = angles(jnp.full((8, 128), 64, jnp.int32), lags[:8])
        tc = jnp.concatenate([jnp.cos(turn)] * 8, axis=0)
        ts = jnp.concatenate([jnp.sin(turn)] * 8, axis=0)
        columns = pl.ds(pl.multiple_of(cb * 128, 128), 128)

        def rotate(q, state):
            c, s = state
            for i in range(CW // 64):
                table[q, i * 64 : (i + 1) * 64, columns] = c.astype(BF16)
                table[q, CW + i * 64 : CW + (i + 1) * 64, columns] = (-s).astype(BF16)
                c, s = c * tc - s * ts, s * tc + c * ts
            return c, s

        lax.fori_loop(0, CHUNKS, rotate, (cosines, sines))
        return carry

    lax.fori_loop(0, LAGP // 128, table_column, 0)

    pltpu.make_async_copy(
        ids_all.at[pl.ds(0, RING - 1)], ids_all.at[pl.ds(0, RING - 1)], id_recv_sem
    ).wait()

    def choose(m, carry):
        for side in range(2):
            wanted = ids_all[m, side : side + 1, :]
            station = lax.broadcasted_iota(jnp.int32, (STATIONS, 128), 0)
            hot = jnp.where(station == wanted, F32(1), F32(0))
            sel[side, m] = jnp.transpose(hot)[:PAIRS].astype(BF16)
        return carry

    lax.fori_loop(0, RING, choose, 0)

    def place(t, carry):
        target = lax.broadcasted_iota(jnp.int32, (128, RING * PAIRS), 0) + t * 128
        hot = jnp.where(target == code_ref[0:1, :], F32(1), F32(0)).astype(BF16)
        gsel[pl.ds(pl.multiple_of(t * 128, 128), 128), :] = hot
        return carry

    lax.fori_loop(0, DEVS * 16 // 128, place, 0)

    acc[...] = jnp.zeros_like(acc)

    def chunk(q, carry):
        pltpu.make_async_copy(
            wr.at[q, pl.ds(0, MEMBERS - 1)], wr.at[q, pl.ds(0, MEMBERS - 1)], w_recv_sem.at[q]
        ).wait()

        def repack(i, inner):
            both = wr[q, pl.ds(2 * i, 2)].astype(F32)
            rows = pl.ds(pl.multiple_of(i * 16, 16), 16)
            wc[rows, :CW] = both[:, :8].reshape(16, CW).astype(BF16)
            wc[rows, CW:] = both[:, 8:].reshape(16, CW).astype(BF16)
            return inner

        lax.fori_loop(0, MEMBERS // 2, repack, 0)

        def correlate(m, inner):
            a = jnp.dot(sel[0, m], wc[...], preferred_element_type=F32)
            b = jnp.dot(sel[1, m], wc[...], preferred_element_type=F32)
            a0, a1, b0, b1 = a[:, :CW], a[:, CW:], b[:, :CW], b[:, CW:]
            rows = pl.ds(pl.multiple_of(m * PAIRS, 32), PAIRS)
            cross[rows, :CW] = (a0 * b0 + a1 * b1).astype(BF16)
            cross[rows, CW:] = (a1 * b0 - a0 * b1).astype(BF16)
            return inner

        lax.fori_loop(0, RING, correlate, 0)

        def transform(t, inner):
            columns = pl.ds(pl.multiple_of(t * 256, 256), 256)
            acc[:, columns] += jnp.dot(cross[...], table[q, :, columns], preferred_element_type=F32)
            return inner

        lax.fori_loop(0, LAGP // 256, transform, 0)
        acc[:, LAGP - 128 :] += jnp.dot(
            cross[...], table[q, :, LAGP - 128 :], preferred_element_type=F32
        )
        return carry

    lax.fori_loop(0, CHUNKS, chunk, 0)

    def block(y, c):
        return pl.ds(pl.multiple_of((2 * y + c) * PAIRS, 32), PAIRS)

    a_copies = []
    for i in range(4):
        y = lax.rem(my_y + i + 1, 4)
        a_send[y] = acc[block(y, 1 - my_c), :].astype(BF16)
        copy = pltpu.make_async_remote_copy(
            src_ref=a_send.at[y], dst_ref=a_recv.at[y],
            send_sem=a_send_sem.at[i], recv_sem=a_recv_sem.at[i],
            device_id={"sta": me + 1 - 2 * my_c}, device_id_type=MESH,
        )
        copy.start()
        a_copies.append(copy)
    b_copies = []
    for i in range(3):
        y = lax.rem(my_y + i + 1, 4)
        a_copies[i].wait_recv()
        b_send[i] = (acc[block(y, my_c), :] + a_recv[y].astype(F32)).astype(BF16)
        copy = pltpu.make_async_remote_copy(
            src_ref=b_send.at[i], dst_ref=b_recv.at[i],
            send_sem=b_send_sem.at[i], recv_sem=b_recv_sem.at[i],
            device_id={"sta": row + 2 * y + my_c}, device_id_type=MESH,
        )
        copy.start()
        b_copies.append(copy)
    a_copies[3].wait_recv()
    mine = block(my_y, my_c)
    acc[mine, :] = acc[mine, :] + a_recv[my_y].astype(F32)
    for copy in b_copies:
        copy.wait_recv()
    scale = F32(BINS ** (-0.5))
    for k in range(SEGS):
        width = min(SEG, LAGP - k * SEG)
        cut = slice(k * SEG, k * SEG + width)
        total = acc[mine, cut]
        for i in range(3):
            total = total + b_recv[i, :, cut].astype(F32)
        corr2[k * PAIRS : (k + 1) * PAIRS, :width] = (total * scale).astype(BF16)
        if width < SEG:
            corr2[k * PAIRS : (k + 1) * PAIRS, width:] = jnp.zeros((PAIRS, SEG - width), BF16)
    corr2[SEGS * PAIRS :, :] = slot_ref[...]

    def pack(t, carry):
        rows = pl.ds(pl.multiple_of(t * 256, 256), 256)
        out = jnp.dot(gsel[rows, :], corr2[...], preferred_element_type=F32)
        c_send[pl.ds(t * 16, 16)] = out.reshape(16, 16, SEG).astype(BF16)
        return carry

    lax.fori_loop(0, DEVS // 16, pack, 0)
    own = pltpu.make_async_copy(c_send.at[dev], got_ref.at[dev], own_sem)
    own.start()

    def route(i, carry):
        peer = lax.rem(dev + i, DEVS)
        pltpu.make_async_remote_copy(
            src_ref=c_send.at[peer], dst_ref=got_ref.at[dev],
            send_sem=c_send_sem, recv_sem=c_recv_sem,
            device_id={"grp": peer // MEMBERS, "sta": lax.rem(peer, MEMBERS)},
            device_id_type=MESH,
        ).start()
        return carry

    lax.fori_loop(1, DEVS, route, 0)

    for i in range(4):
        a_copies[i].wait_send()
    for i in range(3):
        b_copies[i].wait_send()
    pltpu.make_async_copy(
        ids_all.at[pl.ds(0, RING - 1)], ids_all.at[pl.ds(0, RING - 1)], id_send_sem
    ).wait()

    def sent(q, carry):
        pltpu.make_async_copy(
            wr.at[q, pl.ds(0, MEMBERS - 1)], wr.at[q, pl.ds(0, MEMBERS - 1)], w_send_sem.at[q]
        ).wait()
        return carry

    lax.fori_loop(0, CHUNKS, sent, 0)
    own.wait()
    rest = c_send.at[pl.ds(0, DEVS - 1)]
    pltpu.make_async_copy(rest, rest, c_send_sem).wait()
    pltpu.make_async_copy(rest, rest, c_recv_sem).wait()


def correlate_and_route(x, ids, code, slots):
    vmem = pl.BlockSpec(memory_space=pltpu.VMEM)
    dma = pltpu.SemaphoreType.DMA
    return pl.pallas_call(
        main_kernel,
        out_shape=jax.ShapeDtypeStruct((DEVS, 16, SEG), BF16),
        in_specs=[vmem] * 4,
        out_specs=pl.BlockSpec(memory_space=pl.ANY),
        scratch_shapes=[
            pltpu.VMEM((RING, CHUNKS, 16, CW), BF16),
            pltpu.VMEM((CHUNKS, MEMBERS, 16, CW), BF16),
            pltpu.VMEM((STATIONS, 2 * CW), BF16),
            pltpu.VMEM((RING, 8, 128), jnp.int32),
            pltpu.VMEM((2, RING, PAIRS, STATIONS), BF16),
            pltpu.VMEM((CHUNKS, 2 * CW, LAGP), BF16),
            pltpu.VMEM((RING * PAIRS, LAGP), F32),
            pltpu.VMEM((RING * PAIRS, 2 * CW), BF16),
            pltpu.VMEM((4, PAIRS, LAGP), BF16),
            pltpu.VMEM((4, PAIRS, LAGP), BF16),
            pltpu.VMEM((3, PAIRS, LAGP), BF16),
            pltpu.VMEM((3, PAIRS, LAGP), BF16),
            pltpu.VMEM((RING * PAIRS, SEG), BF16),
            pltpu.VMEM((DEVS * 16, RING * PAIRS), BF16),
            pltpu.VMEM((DEVS, 16, SEG), BF16),
            dma, dma,
            dma((CHUNKS,)), dma((CHUNKS,)),
            dma((4,)), dma((4,)),
            dma((3,)), dma((3,)),
            dma, dma, dma,
        ],
        compiler_params=pltpu.CompilerParams(
            collective_id=0, has_side_effects=True, vmem_limit_bytes=60 * 1024 * 1024
        ),
    )(x, ids, code, slots)


def stack_kernel(got_ref, stacks_ref, out_ref):
    rows = DEVS * 16
    got = got_ref[...].reshape(rows, SEG)
    first = jnp.where(lax.broadcasted_iota(jnp.int32, (8, SEG), 1) == 0, F32(1), F32(0)).astype(BF16)
    marks = lax.dot_general(first, got, (((1,), (1,)), ((), ())), preferred_element_type=F32)
    place = lax.broadcasted_iota(jnp.int32, (8, rows), 1) & 15

    def spread(values, offset):
        def back(v, n):
            return pltpu.roll(v, rows - n, 1)

        values = back(values, offset)
        values = jnp.maximum(values, back(values, 1))
        values = jnp.maximum(values, back(values, 2))
        return jnp.maximum(values, back(values, 3))

    slots = jnp.maximum(
        spread(jnp.where(place == 14, marks, F32(0)), 8),
        spread(jnp.where(place == 15, marks, F32(0)), 2),
    )
    segment = jnp.where(place < 7, place, place - 7)
    code = jnp.where(place < 14, slots.astype(jnp.int32) + segment * PAIRS, -1)[0:1]
    for k in range(SEGS):
        want = lax.broadcasted_iota(jnp.int32, (PAIRS, rows), 0) + k * PAIRS
        hot = jnp.where(want == code, F32(1), F32(0)).astype(BF16)
        part = jnp.dot(hot, got, preferred_element_type=F32)
        width = min(SEG, LAGS - k * SEG)
        cut = slice(k * SEG, k * SEG + width)
        out_ref[:, cut] = stacks_ref[:, cut] + part[:, :width]


def add_rows(got, stacks):
    vmem = pl.BlockSpec(memory_space=pltpu.VMEM)
    return pl.pallas_call(
        stack_kernel,
        out_shape=jax.ShapeDtypeStruct(stacks.shape, F32),
        in_specs=[vmem] * 2,
        out_specs=vmem,
        compiler_params=pltpu.CompilerParams(vmem_limit_bytes=40 * 1024 * 1024),
    )(got, stacks)


def local(spectra, stacks, pair_sta, pair_valid, owner, slot):
    x = jnp.transpose(spectra, (1, 0, 2))
    ids = jnp.pad(pair_sta, ((0, 6), (0, 128 - PAIRS)))
    dest = owner[:, 0]
    order = lax.iota(jnp.int32, PAIRS)
    same = (dest[:, None] == dest[None, :]) & (order[:, None] < order[None, :])
    position = jnp.sum(same.astype(jnp.int32), axis=0)
    base = dest * 16
    code = (base + position * 7)[None, :] + lax.iota(jnp.int32, SEGS)[:, None]
    code = jnp.where(pair_valid[None, :] == 1, code, -1)
    code = jnp.concatenate([code, (base + 14 + position)[None, :]], axis=0).reshape(1, RING * PAIRS)
    code = jnp.broadcast_to(code, (8, RING * PAIRS))
    slots = jnp.broadcast_to(slot.astype(BF16)[:, None], (PAIRS, SEG))
    got = correlate_and_route(x, ids, code, slots)
    return add_rows(got, stacks)


def solution(mesh):
    return jax.shard_map(
        local,
        mesh=mesh,
        in_specs=(
            P(("grp", "sta"), None, None),
            P(("grp", "sta"), None),
            P(None, ("grp", "sta")),
            P(("grp", "sta")),
            P(("grp", "sta"), None),
            P(("grp", "sta")),
        ),
        out_specs=P(("grp", "sta"), None),
        check_vma=False,
    )
```

time: 1230 us -> 107 us (0.09)
  matrix products: 972 us -> 0 us
  Pallas kernels: 0 us -> 95.9 us
  waiting for transfers between devices: 94.5 us -> 0 us
  local copies, waits for them, and re-layouts: 73.5 us -> 6.84 us
  other arithmetic: 27.4 us -> 3.48 us
  loops' own time: 20.3 us -> 0 us
  starting transfers between devices: 18.8 us -> 0 us
  between operations: 14 us -> 0.03 us
    dot_general x20 -> x0, matrix products: 972 us -> none  [the longest x9 487 us: add_block(): return total + jnp.dot(imag_part, sines, preferred_element_type=jnp.float32)]
    pallas_call x0 -> x2, Pallas kernels: none -> 95.9 us  [the longest x1 93.2 us: correlate_and_route(): pl.pallas_call(main_kernel, out_shape=jax.ShapeDtypeStruct((DEVS, 16, SEG...]
    all_gather x1 -> x0, waiting for transfers between devices: 68.5 us -> none  [local(): gathered = lax.all_gather(whitened, 'sta', axis=0, tiled=True)]
    gather x2 -> x0, local copies, waits for them, and re-layouts: 46.6 us -> none  [the longest x1 23.4 us: local(): first = jnp.take(gathered, pair_sta[0], axis=0)]
    all_to_all x2 -> x0, waiting for transfers between devices: 26 us -> none  [joined_exchange(): tiles = lax.all_to_all(tiles, axis, split_axis=0, concat_axis=0, tiled=True)]
    dynamic_slice x9 -> x0, local copies, waits for them, and re-layouts: 22.1 us -> none  [add_block(): lax.dynamic_slice_in_dim(second, start, fblock, 2).astype(jnp.float32)]
    another operation x1 -> x0, loops' own time: 20.3 us -> none  [local(): lax.fori_loop(0, total_bins // fblock, add_block, jnp.zeros((pair_count,...]
    all_to_all x2 -> x0, starting transfers between devices: 18.7 us -> none  [joined_exchange(): tiles = lax.all_to_all(tiles, axis, split_axis=0, concat_axis=0, tiled=True)]
  transfers between devices with their start and end apart: 3 -> 0, of which waited for: 2 -> 0; matrix products, arithmetic and copies ran while one was open for 87% -> 0% of each run, Pallas kernels for 0% -> 0%
where the time goes in v1:
time: 107 us; the launch traced here: 106 us
  Pallas kernels  95.9 us (90%)
  local copies, waits for them, and re-layouts  6.84 us (6%)
  other arithmetic  3.48 us (3%)
    pallas_call x1, Pallas kernels, correlate_and_route(): pl.pallas_call(main_kernel, out_shape=jax.ShapeDtypeStruct((DEVS, 16, SEG...  93.2 us
    unnamed x5, local copies, waits for them, and re-layouts  4.19 us
    pallas_call x1, Pallas kernels, add_rows(): pl.pallas_call(stack_kernel, out_shape=jax.ShapeDtypeStruct(stacks.shape,...  2.74 us

profile of v1, /device:TPU:1, one launch (start us, length us, event | category | flops | bytes accessed | tf_op | source)
XLA Modules:
  0.0 106.2 jit_solution(3978756183774355930)
XLA Ops:
  0.0 0.8 convert_reduce_fusion
  0.8 0.7 bitcast_add_fusion
  1.5 0.7 multiply_add_fusion
  2.1 0.7 broadcast_compare_fusion
  2.8 0.7 convert_element_type.7
  3.5 0.1 broadcast_in_dim.20
  3.6 1.3 %pad.4.ids_ref = s32[8,128]{1,0:T(8,128)} pad(s32[2,96]{1,0:T(2,128)} %param.8, s32[]{:T(128)} %constant.0.clone.1), padding=0_6x0_32 | pad | bytes 4868 | tf_op jit(solution)/shard_map/jit(_pad)/pad | solution.py:373
  4.8 0.6 broadcast_in_dim.34.code_ref
  5.4 0.7 broadcast_in_dim.35.slot_ref
  6.1 3.0 %copy.10 = f32[8,2,18432]{2,0,1:T(8,128)} copy(f32[8,2,18432]{2,1,0:T(2,128)} %param.6) | data formatting | bytes 2359296 | tf_op args[0]
  9.1 0.0 copy-start.1
  9.1 93.2 %shard_map.64.got_ref = bf16[128,16,256]{2,1,0:T(8,128)(2,1)} custom-call(f32[2,8,18432]{2,1,0:T(8,128)} %bitcast.9, s32[8,128]{1,0:T(8,128)} %pad.4.ids_ref, s32[8,768]{1,0:T(8,128)} %broadcast_in_dim.34.code_ref, bf16[96,256]{1,0:T(8,128)(2,1)} %broadcast_in_dim.35.slot_ref), custom_call_target="tpu_custom_call" | custom-call | tf_op jit(solution)/shard_map/pallas_call | solution.py:296
  102.3 0.0 copy-done.1
  102.3 0.0 copy-start
  102.3 1.2 %copy-done = bf16[128,16,256]{2,1,0:T(8,128)(2,1)S(1)} copy-done((bf16[128,16,256]{2,1,0:T(8,128)(2,1)S(1)}, bf16[128,16,256]{2,1,0:T(8,128)(2,1)}, u32[]{:S(2)}) %copy-start) | copy-done | bytes 1048600
  103.5 2.7 %shard_map.65 = f32[96,1601]{1,0:T(8,128)} custom-call(bf16[128,16,256]{2,1,0:T(8,128)(2,1)S(1)} %copy-done, f32[96,1601]{1,0:T(8,128)S(1)} %copy-done.1), custom_call_target="tpu_custom_call" | custom-call | tf_op jit(solution)/shard_map/pallas_call | solution.py:362
  (2 shorter events, 0.0 us)
Async XLA Ops:
  9.1 93.2 %copy-start.1 = (f32[96,1601]{1,0:T(8,128)S(1)}, f32[96,1601]{1,0:T(8,128)}, u32[]{:S(2)}) copy-start(f32[96,1601]{1,0:T(8,128)} %stacks_ref.1) | copy-start | bytes 1844356
  102.3 1.2 %copy-start = (bf16[128,16,256]{2,1,0:T(8,128)(2,1)S(1)}, bf16[128,16,256]{2,1,0:T(8,128)(2,1)}, u32[]{:S(2)}) copy-start(bf16[128,16,256]{2,1,0:T(8,128)(2,1)} %shard_map.64.got_ref) | copy-start | bytes 3145732

commit v2 on v1

v2 whole, which is shorter than its diff:
```python
import functools
import math

import jax
import jax.numpy as jnp
from jax import lax
from jax.experimental import pallas as pl
from jax.experimental.pallas import tpu as pltpu
from jax.sharding import PartitionSpec as P

BAND = 64
MESH = pl.DeviceIdType.MESH
BF16 = jnp.bfloat16
F32 = jnp.float32

BINS = 18432
LAGS = 1601
HALF = (LAGS + 1) // 2
SIDE = 832
COLS = 2 * SIDE
PAIRS = 96
RING = 8
SLAB = BINS // RING
WIDTHS = (768, 768, 512, 256)
STARTS = (0, 768, 1536, 2048)
PARTS = len(WIDTHS)
MEMBERS = 32
GROUPS = 4
DEVS = 128
STATIONS = 256
SEG = 256
SEGS = 7


def angles(freqs, shifts):
    product = (freqs * shifts).astype(F32)
    turns = jnp.floor(product * F32(1.0 / (2 * BINS)))
    return (product - turns * F32(2 * BINS)) * F32(math.pi / BINS)


def main_kernel(x_ref, meta_ref, got_ref, *scratch):
    ws, wr = scratch[:PARTS], scratch[PARTS : 2 * PARTS]
    (
        wc, ids_all, sel, tcos, tsin, acc, cross, a_send, a_recv, b_send, b_recv,
        corr2, gsel, c_send,
        id_send_sem, id_recv_sem, w_send_sem, w_recv_sem,
        a_send_sem, a_recv_sem, b_send_sem, b_recv_sem, c_send_sem, c_recv_sem, own_sem,
    ) = scratch[2 * PARTS :]
    grp = lax.axis_index("grp")
    me = lax.axis_index("sta")
    dev = grp * MEMBERS + me
    my_slab = lax.rem(me, RING)
    row = me - my_slab
    my_y = my_slab // 2
    my_c = lax.rem(my_slab, 2)

    barrier = pltpu.get_barrier_semaphore()

    def greet(i, carry):
        peer = lax.rem(dev + i, DEVS)
        pl.semaphore_signal(
            barrier, inc=1,
            device_id={"grp": peer // MEMBERS, "sta": lax.rem(peer, MEMBERS)},
            device_id_type=MESH,
        )
        return carry

    lax.fori_loop(1, DEVS, greet, 0)

    lane = lax.broadcasted_iota(jnp.int32, (128, 128), 1) // BAND
    sub = lax.broadcasted_iota(jnp.int32, (128, 128), 0) // BAND
    bands = jnp.where(lane == sub, F32(1), F32(0))

    def whiten(s, carry):
        base = pl.multiple_of(s * SLAB, 128)
        x0 = x_ref[:, 0, pl.ds(base, SLAB)]
        x1 = x_ref[:, 1, pl.ds(base, SLAB)]
        square = x0 * x0 + x1 * x1
        tiles = SLAB // 128
        rows = jnp.concatenate([square[:, j * 128 : (j + 1) * 128] for j in range(tiles)], axis=0)
        power = jnp.dot(
            rows, bands, precision=lax.Precision.HIGHEST, preferred_element_type=F32
        ) * F32(1.0 / (2 * BAND))
        inverse = lax.rsqrt(power + F32(1e-06))
        for j in range(tiles):
            inv = inverse[j * 8 : (j + 1) * 8]
            cut = slice(j * 128, (j + 1) * 128)
            both = jnp.concatenate([x0[:, cut] * inv, x1[:, cut] * inv], axis=0).astype(BF16)
            q = max(p for p in range(PARTS) if STARTS[p] <= j * 128)
            o = j * 128 - STARTS[q]
            ws[q][s, :, o : o + 128] = both
        return carry

    lax.fori_loop(0, RING, whiten, 0)
    pl.semaphore_wait(barrier, DEVS - 1)

    def send_ids(i, carry):
        peer = row + lax.rem(my_slab + i, RING)
        pltpu.make_async_remote_copy(
            src_ref=meta_ref, dst_ref=ids_all.at[my_slab],
            send_sem=id_send_sem, recv_sem=id_recv_sem,
            device_id={"sta": peer}, device_id_type=MESH,
        ).start()
        return carry

    lax.fori_loop(1, RING, send_ids, 0)
    ids_all[my_slab] = meta_ref[...]

    def send_part(q):
        def one(i, carry):
            peer = lax.rem(me + i, MEMBERS)
            pltpu.make_async_remote_copy(
                src_ref=ws[q].at[lax.rem(peer, RING)], dst_ref=wr[q].at[me],
                send_sem=w_send_sem.at[q], recv_sem=w_recv_sem.at[q],
                device_id={"sta": peer}, device_id_type=MESH,
            ).start()
            return carry

        lax.fori_loop(1, MEMBERS, one, 0)
        wr[q][me] = ws[q][my_slab]

    for q in range(PARTS):
        send_part(q)

    start = my_slab * SLAB

    def table_column(cb, half):
        column = lax.broadcasted_iota(jnp.int32, (64, 128), 1) + cb * 128
        cosine_side = column < SIDE
        lags = jnp.where(cosine_side, column, column - SIDE)
        freqs = lax.broadcasted_iota(jnp.int32, (64, 128), 0) + start
        theta = angles(freqs, lags)
        cosines, sines = jnp.cos(theta), jnp.sin(theta)
        turn = angles(jnp.full((8, 128), 64, jnp.int32), lags[:8])
        tc = jnp.concatenate([jnp.cos(turn)] * 8, axis=0)
        ts = jnp.concatenate([jnp.sin(turn)] * 8, axis=0)

        def rotate(i, state):
            c, s = state
            for step in range(4):
                rows = pl.ds(pl.multiple_of(i * 256 + step * 64, 64), 64)
                if half == "both":
                    tcos[rows, SIDE - 64 : SIDE + 64] = jnp.where(cosine_side, c, F32(0)).astype(BF16)
                    tsin[rows, :128] = jnp.where(cosine_side, F32(0), -s).astype(BF16)
                elif half == "cos":
                    tcos[rows, pl.ds(pl.multiple_of(cb * 128, 128), 128)] = c.astype(BF16)
                else:
                    tsin[rows, pl.ds(pl.multiple_of(cb * 128 - 768, 128), 128)] = (-s).astype(BF16)
                c, s = c * tc - s * ts, s * tc + c * ts
            return c, s

        lax.fori_loop(0, SLAB // 256, rotate, (cosines, sines))

    def cosine_column(cb, carry):
        table_column(cb, "cos")
        return carry

    def sine_column(cb, carry):
        table_column(cb, "sin")
        return carry

    lax.fori_loop(0, 6, cosine_column, 0)
    table_column(6, "both")
    lax.fori_loop(7, 13, sine_column, 0)

    pltpu.make_async_copy(
        ids_all.at[pl.ds(0, RING - 1)], ids_all.at[pl.ds(0, RING - 1)], id_recv_sem
    ).wait()

    def choose(m, carry):
        station = lax.broadcasted_iota(jnp.int32, (STATIONS, 128), 0)
        for side in range(2):
            wanted = ids_all[m, side : side + 1, :]
            hot = jnp.transpose(jnp.where(station == wanted, F32(1), F32(0))).astype(BF16)
            for i in range(PAIRS // 16):
                sel[m, i * 32 + side * 16 : i * 32 + side * 16 + 16, :] = hot[i * 16 : (i + 1) * 16]
        return carry

    lax.fori_loop(0, RING, choose, 0)

    for q in range(PARTS):
        width = WIDTHS[q]
        arrived = wr[q].at[pl.ds(0, MEMBERS - 1)]
        pltpu.make_async_copy(arrived, arrived, w_recv_sem.at[q]).wait()

        def repack(i, carry):
            both = wr[q][pl.ds(2 * i, 2)].astype(F32)
            rows = pl.ds(pl.multiple_of(i * 16, 16), 16)
            low = both[:, :8].reshape(16, width).astype(BF16)
            high = both[:, 8:].reshape(16, width).astype(BF16)
            for j in range(width // 128):
                wc[j, rows, :128] = low[:, j * 128 : (j + 1) * 128]
                wc[j, rows, 128:] = high[:, j * 128 : (j + 1) * 128]
            return carry

        lax.fori_loop(0, MEMBERS // 2, repack, 0)

        def correlate(j, carry):
            real_at = pl.ds(pl.multiple_of(j * 128, 128), 128)
            imag_at = pl.ds(pl.multiple_of(768 + j * 128, 128), 128)
            for m in range(0, RING, 4):
                both = jnp.dot(
                    sel[m : m + 4].reshape(4 * 2 * PAIRS, STATIONS), wc[j], preferred_element_type=F32
                )
                for i in range(4 * PAIRS // 16):
                    a0, a1 = both[i * 32 : i * 32 + 16, :128], both[i * 32 : i * 32 + 16, 128:]
                    b0, b1 = both[i * 32 + 16 : i * 32 + 32, :128], both[i * 32 + 16 : i * 32 + 32, 128:]
                    rows = slice(m * PAIRS + i * 16, m * PAIRS + i * 16 + 16)
                    cross[rows, real_at] = (a0 * b0 + a1 * b1).astype(BF16)
                    cross[rows, imag_at] = (a1 * b0 - a0 * b1).astype(BF16)
            return carry

        lax.fori_loop(0, width // 128, correlate, 0)

        bins = slice(STARTS[q], STARTS[q] + width)

        def add(columns, value):
            if q == 0:
                acc[:, columns] = value
            else:
                acc[:, columns] += value

        def transform(t, carry):
            left = pl.ds(pl.multiple_of(t * 256, 256), 256)
            right = pl.ds(pl.multiple_of(t * 256 + 128, 128), 256)
            far = pl.ds(pl.multiple_of(t * 256 + 896, 128), 256)
            add(left, jnp.dot(cross[:, :width], tcos[bins, left], preferred_element_type=F32))
            add(far, jnp.dot(cross[:, 768 : 768 + width], tsin[bins, right], preferred_element_type=F32))
            return carry

        lax.fori_loop(0, 3, transform, 0)
        add(
            slice(768, 896),
            jnp.dot(cross[:, :width], tcos[bins, 768:], preferred_element_type=F32)
            + jnp.dot(cross[:, 768 : 768 + width], tsin[bins, :128], preferred_element_type=F32),
        )

    def block(y, c):
        return pl.ds(pl.multiple_of((2 * y + c) * PAIRS, 32), PAIRS)

    a_copies = []
    for i in range(4):
        y = lax.rem(my_y + i + 1, 4)
        a_send[y] = acc[block(y, 1 - my_c), :].astype(BF16)
        copy = pltpu.make_async_remote_copy(
            src_ref=a_send.at[y], dst_ref=a_recv.at[y],
            send_sem=a_send_sem.at[i], recv_sem=a_recv_sem.at[i],
            device_id={"sta": me + 1 - 2 * my_c}, device_id_type=MESH,
        )
        copy.start()
        a_copies.append(copy)
    meta = meta_ref[...]
    square = (128, 128)
    sub, lane = lax.broadcasted_iota(jnp.int32, square, 0), lax.broadcasted_iota(jnp.int32, square, 1)
    dest = meta[3:4, :]
    dest_across = jnp.transpose(jnp.broadcast_to(dest.astype(F32), square)).astype(jnp.int32)
    earlier = (dest_across == dest) & (sub < lane) & (sub < PAIRS)
    position = jnp.sum(jnp.where(earlier, F32(1), F32(0)), axis=0, keepdims=True).astype(jnp.int32)
    real_pair = lane[0:1] < PAIRS
    counted = real_pair & (meta[2:3, :] == 1)
    row_code = jnp.where(counted, dest * 16 + position * SEGS, -64)
    slot_code = jnp.where(real_pair, dest * 16 + 2 * SEGS + position, -64)

    def place(t, carry):
        target = lax.broadcasted_iota(jnp.int32, (128, 128), 0) + t * 128
        rows = pl.ds(pl.multiple_of(t * 128, 128), 128)
        for k in range(SEGS + 1):
            code = slot_code if k == SEGS else row_code + k
            gsel[rows, k * 128 : (k + 1) * 128] = jnp.where(target == code, F32(1), F32(0)).astype(BF16)
        return carry

    lax.fori_loop(0, DEVS * 16 // 128, place, 0)
    slot_across = jnp.transpose(jnp.broadcast_to(meta[4:5, :].astype(F32), square)).astype(BF16)
    corr2[SEGS * 128 :, :128] = slot_across
    corr2[SEGS * 128 :, 128:] = slot_across

    b_copies = []
    for i in range(3):
        y = lax.rem(my_y + i + 1, 4)
        a_copies[i].wait_recv()
        b_send[i] = (acc[block(y, my_c), :] + a_recv[y].astype(F32)).astype(BF16)
        copy = pltpu.make_async_remote_copy(
            src_ref=b_send.at[i], dst_ref=b_recv.at[i],
            send_sem=b_send_sem.at[i], recv_sem=b_recv_sem.at[i],
            device_id={"sta": row + 2 * y + my_c}, device_id_type=MESH,
        )
        copy.start()
        b_copies.append(copy)
    a_copies[3].wait_recv()
    mine = block(my_y, my_c)
    acc[mine, :] = acc[mine, :] + a_recv[my_y].astype(F32)
    for copy in b_copies:
        copy.wait_recv()
    scale = F32(BINS ** (-0.5))
    for k in range(SEGS):
        width = min(SEG, COLS - k * SEG)
        cut = slice(k * SEG, k * SEG + width)
        total = acc[mine, cut]
        for i in range(3):
            total = total + b_recv[i, :, cut].astype(F32)
        corr2[k * 128 : k * 128 + PAIRS, :width] = (total * scale).astype(BF16)
        corr2[k * 128 + PAIRS : (k + 1) * 128, :] = jnp.zeros((128 - PAIRS, SEG), BF16)
        if width < SEG:
            corr2[k * 128 : k * 128 + PAIRS, width:] = jnp.zeros((PAIRS, SEG - width), BF16)

    def pack(t, carry):
        rows = pl.ds(pl.multiple_of(t * 256, 256), 256)
        out = jnp.dot(gsel[rows, :], corr2[...], preferred_element_type=F32)
        c_send[pl.ds(t * 16, 16)] = out.reshape(16, 16, SEG).astype(BF16)
        return carry

    lax.fori_loop(0, DEVS // 16, pack, 0)
    own = pltpu.make_async_copy(c_send.at[dev], got_ref.at[dev], own_sem)
    own.start()

    def route(i, carry):
        peer = lax.rem(dev + i, DEVS)
        pltpu.make_async_remote_copy(
            src_ref=c_send.at[peer], dst_ref=got_ref.at[dev],
            send_sem=c_send_sem, recv_sem=c_recv_sem,
            device_id={"grp": peer // MEMBERS, "sta": lax.rem(peer, MEMBERS)},
            device_id_type=MESH,
        ).start()
        return carry

    lax.fori_loop(1, DEVS, route, 0)

    for i in range(4):
        a_copies[i].wait_send()
    for i in range(3):
        b_copies[i].wait_send()
    pltpu.make_async_copy(
        ids_all.at[pl.ds(0, RING - 1)], ids_all.at[pl.ds(0, RING - 1)], id_send_sem
    ).wait()

    for q in range(PARTS):
        sent = wr[q].at[pl.ds(0, MEMBERS - 1)]
        pltpu.make_async_copy(sent, sent, w_send_sem.at[q]).wait()
    own.wait()
    rest = c_send.at[pl.ds(0, DEVS - 1)]
    pltpu.make_async_copy(rest, rest, c_send_sem).wait()
    pltpu.make_async_copy(rest, rest, c_recv_sem).wait()


def correlate_and_route(x, meta):
    vmem = pl.BlockSpec(memory_space=pltpu.VMEM)
    dma = pltpu.SemaphoreType.DMA
    return pl.pallas_call(
        main_kernel,
        out_shape=jax.ShapeDtypeStruct((DEVS, 16, SEG), BF16),
        in_specs=[vmem] * 2,
        out_specs=pl.BlockSpec(memory_space=pl.ANY),
        scratch_shapes=[
            *[pltpu.VMEM((RING, 16, w), BF16) for w in WIDTHS],
            *[pltpu.VMEM((MEMBERS, 16, w), BF16) for w in WIDTHS],
            pltpu.VMEM((max(WIDTHS) // 128, STATIONS, 256), BF16),
            pltpu.VMEM((RING, 8, 128), jnp.int32),
            pltpu.VMEM((RING, 2 * PAIRS, STATIONS), BF16),
            pltpu.VMEM((SLAB, 896), BF16),
            pltpu.VMEM((SLAB, 896), BF16),
            pltpu.VMEM((RING * PAIRS, COLS), F32),
            pltpu.VMEM((RING * PAIRS, 2 * max(WIDTHS)), BF16),
            pltpu.VMEM((4, PAIRS, COLS), BF16),
            pltpu.VMEM((4, PAIRS, COLS), BF16),
            pltpu.VMEM((3, PAIRS, COLS), BF16),
            pltpu.VMEM((3, PAIRS, COLS), BF16),
            pltpu.VMEM(((SEGS + 1) * 128, SEG), BF16),
            pltpu.VMEM((DEVS * 16, (SEGS + 1) * 128), BF16),
            pltpu.VMEM((DEVS, 16, SEG), BF16),
            dma, dma,
            dma((PARTS,)), dma((PARTS,)),
            dma((4,)), dma((4,)),
            dma((3,)), dma((3,)),
            dma, dma, dma,
        ],
        compiler_params=pltpu.CompilerParams(
            collective_id=0, has_side_effects=True, vmem_limit_bytes=46 * 1024 * 1024
        ),
    )(x, meta)


def stack_kernel(got_ref, stacks_ref, out_ref):
    rows = DEVS * 16
    got = got_ref[...].reshape(rows, SEG)
    first = jnp.where(lax.broadcasted_iota(jnp.int32, (8, SEG), 1) == 0, F32(1), F32(0)).astype(BF16)
    marks = lax.dot_general(first, got, (((1,), (1,)), ((), ())), preferred_element_type=F32)
    place = lax.broadcasted_iota(jnp.int32, (8, rows), 1) & 15

    def spread(values, offset):
        def back(v, n):
            return pltpu.roll(v, rows - n, 1)

        values = back(values, offset)
        values = jnp.maximum(values, back(values, 1))
        values = jnp.maximum(values, back(values, 2))
        return jnp.maximum(values, back(values, 3))

    slots = jnp.maximum(
        spread(jnp.where(place == 14, marks, F32(0)), 8),
        spread(jnp.where(place == 15, marks, F32(0)), 2),
    )
    segment = jnp.where(place < 7, place, place - 7)
    code = jnp.where(place < 14, slots.astype(jnp.int32) + segment * PAIRS, -1)[0:1]
    parts = []
    for k in range(SEGS):
        want = lax.broadcasted_iota(jnp.int32, (PAIRS, rows), 0) + k * PAIRS
        hot = jnp.where(want == code, F32(1), F32(0)).astype(BF16)
        parts.append(jnp.dot(hot, got, preferred_element_type=F32))
    sums = jnp.concatenate(parts, axis=1)
    even, odd = sums[:, :896], sums[:, SIDE : SIDE + 896]
    tiles = 7
    gap = even - odd
    high = gap.astype(BF16)
    low = (gap - high.astype(F32)).astype(BF16)
    stack = jnp.concatenate(
        [v[:, t * 128 : (t + 1) * 128] for v in (high, low) for t in range(tiles)], axis=0
    )
    mirror = lax.broadcasted_iota(jnp.int32, (128, 128), 0) + lax.broadcasted_iota(jnp.int32, (128, 128), 1)
    mirror = jnp.where(mirror == 127, F32(1), F32(0)).astype(BF16)
    turned = jnp.dot(stack, mirror, preferred_element_type=F32)
    turned = turned[: tiles * PAIRS] + turned[tiles * PAIRS :]
    behind = jnp.concatenate(
        [turned[t * PAIRS : (t + 1) * PAIRS] for t in reversed(range(tiles))], axis=1
    )
    skip = tiles * 128 - HALF
    out_ref[:, :HALF] = stacks_ref[:, :HALF] + behind[:, skip:]
    out_ref[:, HALF:] = stacks_ref[:, HALF:] + (even + odd)[:, 1:HALF]


def add_rows(got, stacks):
    vmem = pl.BlockSpec(memory_space=pltpu.VMEM)
    return pl.pallas_call(
        stack_kernel,
        out_shape=jax.ShapeDtypeStruct(stacks.shape, F32),
        in_specs=[vmem] * 2,
        out_specs=vmem,
        compiler_params=pltpu.CompilerParams(vmem_limit_bytes=40 * 1024 * 1024),
    )(got, stacks)


def local(spectra, stacks, pair_sta, pair_valid, owner, slot):
    rows = [pair_sta, pair_valid[None, :], owner.reshape(1, PAIRS), slot[None, :]]
    meta = jnp.pad(jnp.concatenate(rows, axis=0), ((0, 3), (0, 128 - PAIRS)))
    got = correlate_and_route(spectra, meta)
    return add_rows(got, stacks)


def solution(mesh):
    return jax.shard_map(
        local,
        mesh=mesh,
        in_specs=(
            P(("grp", "sta"), None, None),
            P(("grp", "sta"), None),
            P(None, ("grp", "sta")),
            P(("grp", "sta")),
            P(("grp", "sta"), None),
            P(("grp", "sta")),
        ),
        out_specs=P(("grp", "sta"), None),
        check_vma=False,
    )
```

time: 107 us -> 86.5 us (0.81)
  Pallas kernels: 95.9 us -> 84.3 us
  local copies, waits for them, and re-layouts: 6.84 us -> 1.27 us
  other arithmetic: 3.48 us -> 0.74 us
    pallas_call x1, Pallas kernels: 93.2 us -> 81.2 us  [correlate_and_route(): pl.pallas_call(main_kernel, out_shape=jax.ShapeDtypeStruct((DEVS, 16, SEG...]
    unnamed x5 -> x4, local copies, waits for them, and re-layouts: 4.19 us -> 1.27 us
    broadcast_in_dim x3 -> x0, local copies, waits for them, and re-layouts: 1.38 us -> none  [the longest x1 0.7 us: local(): slots = jnp.broadcast_to(slot.astype(BF16)[:, None], (PAIRS, SEG))]
    add x2 -> x0, other arithmetic: 1.32 us -> none  [the longest x1 0.66 us: local(): base + 14 + position]
    pad x1, local copies, waits for them, and re-layouts: 1.28 us -> 0.01 us  [local(): meta = jnp.pad(jnp.concatenate(rows, axis=0), ((0, 3), (0, 128 - PAIRS)))]
where the time goes in v2:
time: 86.5 us; the launch traced here: 86.3 us
  Pallas kernels  84.3 us (97%)
  local copies, waits for them, and re-layouts  1.27 us (1%)
    pallas_call x1, Pallas kernels, correlate_and_route(): pl.pallas_call(main_kernel, out_shape=jax.ShapeDtypeStruct((DEVS, 16, SEG...  81.2 us
    pallas_call x1, Pallas kernels, add_rows(): pl.pallas_call(stack_kernel, out_shape=jax.ShapeDtypeStruct(stacks.shape,...  3.04 us

profile of v2, /device:TPU:1, one launch (start us, length us, event | category | flops | bytes accessed | tf_op | source)
XLA Modules:
  0.0 86.3 jit_solution(9696934649982235067)
XLA Ops:
  0.0 0.7 pad_add_fusion
  0.7 0.0 copy-start
  0.8 1.3 %copy-done = f32[8,2,18432]{2,1,0:T(2,128)S(1)} copy-done((f32[8,2,18432]{2,1,0:T(2,128)S(1)}, f32[8,2,18432]{2,1,0:T(2,128)}, u32[]{:S(2)}) %copy-start) | copy-done | bytes 1179672
  2.0 0.0 copy-start.1
  2.0 81.2 %shard_map.64.got_ref = bf16[128,16,256]{2,1,0:T(8,128)(2,1)S(1)} custom-call(f32[8,2,18432]{2,1,0:T(2,128)S(1)} %copy-done, s32[8,128]{1,0:T(8,128)S(1)} %pad.4.meta_ref), custom_call_target="tpu_custom_call" | custom-call | tf_op jit(solution)/shard_map/pallas_call | solution.py:348
  83.3 0.0 copy-done.1
  83.3 3.0 %shard_map.65 = f32[96,1601]{1,0:T(8,128)} custom-call(bf16[128,16,256]{2,1,0:T(8,128)(2,1)S(1)} %shard_map.64.got_ref, f32[96,1601]{1,0:T(8,128)S(1)} %copy-done.1), custom_call_target="tpu_custom_call" | custom-call | tf_op jit(solution)/shard_map/pallas_call | solution.py:432
  (1 shorter events, 0.0 us)
Async XLA Ops:
  0.7 1.3 %copy-start = (f32[8,2,18432]{2,1,0:T(2,128)S(1)}, f32[8,2,18432]{2,1,0:T(2,128)}, u32[]{:S(2)}) copy-start(f32[8,2,18432]{2,1,0:T(2,128)} %x_ref.1) | copy-start | bytes 3538948
  2.0 81.2 %copy-start.1 = (f32[96,1601]{1,0:T(8,128)S(1)}, f32[96,1601]{1,0:T(8,128)}, u32[]{:S(2)}) copy-start(f32[96,1601]{1,0:T(8,128)} %stacks_ref.1) | copy-start | bytes 1844356

commit v3 on v2

v3 whole, which is shorter than its diff:
```python
import functools
import math

import jax
import jax.numpy as jnp
from jax import lax
from jax.experimental import pallas as pl
from jax.experimental.pallas import tpu as pltpu
from jax.sharding import PartitionSpec as P

BAND = 64
MESH = pl.DeviceIdType.MESH
BF16 = jnp.bfloat16
F32 = jnp.float32

BINS = 18432
LAGS = 1601
HALF = (LAGS + 1) // 2
SIDE = 832
COLS = 2 * SIDE
PAIRS = 96
SHARE = PAIRS // 2
RING = 8
BLOCKS = 2 * RING
SLAB = BINS // RING
WIDTHS = (768, 768, 512, 256)
STARTS = (0, 768, 1536, 2048)
PARTS = len(WIDTHS)
MEMBERS = 32
GROUPS = 4
DEVS = 128
STATIONS = 256
SEG = 256
SEGS = 4
PIECES = ((0, 1024), (1024, 640))


def angles(freqs, shifts):
    product = (freqs * shifts).astype(F32)
    turns = jnp.floor(product * F32(1.0 / (2 * BINS)))
    return (product - turns * F32(2 * BINS)) * F32(math.pi / BINS)


def main_kernel(x_ref, meta_ref, got_a, got_b, *scratch):
    ws, wr = scratch[:PARTS], scratch[PARTS : 2 * PARTS]
    (
        wc, ids_all, sel, tcos, tsin, acc, cross,
        a_send_0, a_send_1, a_recv_0, a_recv_1, b_send_0, b_send_1, b_recv_0, b_recv_1,
        corr_0, corr_1, gsel, c_send_0, c_send_1,
        id_send_sem, id_recv_sem, w_send_sem, w_recv_sem,
        a_send_sem, a_recv_sem, b_send_sem, b_recv_sem, c_send_sem, c_recv_sem, own_sem,
    ) = scratch[2 * PARTS :]
    a_send, a_recv = (a_send_0, a_send_1), (a_recv_0, a_recv_1)
    b_send, b_recv = (b_send_0, b_send_1), (b_recv_0, b_recv_1)
    corr, c_send, got = (corr_0, corr_1), (c_send_0, c_send_1), (got_a, got_b)
    grp = lax.axis_index("grp")
    me = lax.axis_index("sta")
    dev = grp * MEMBERS + me
    my_z, inside = me // RING, lax.rem(me, RING)
    my_y, my_c = inside // 2, lax.rem(inside, 2)

    def slab_of(member):
        z, rest = member // RING, lax.rem(member, RING)
        return 2 * lax.rem(z + rest // 2, 4) + lax.rem(rest, 2)

    my_slab = slab_of(me)
    row = me - inside

    barrier = pltpu.get_barrier_semaphore()

    def greet(i, carry):
        peer = lax.rem(dev + i, DEVS)
        pl.semaphore_signal(
            barrier, inc=1,
            device_id={"grp": peer // MEMBERS, "sta": lax.rem(peer, MEMBERS)},
            device_id_type=MESH,
        )
        return carry

    lax.fori_loop(1, DEVS, greet, 0)

    lane = lax.broadcasted_iota(jnp.int32, (128, 128), 1) // BAND
    sub = lax.broadcasted_iota(jnp.int32, (128, 128), 0) // BAND
    bands = jnp.where(lane == sub, F32(1), F32(0))

    def whiten(s, carry):
        base = pl.multiple_of(s * SLAB, 128)
        x0 = x_ref[:, 0, pl.ds(base, SLAB)]
        x1 = x_ref[:, 1, pl.ds(base, SLAB)]
        square = x0 * x0 + x1 * x1
        tiles = SLAB // 128
        rows = jnp.concatenate([square[:, j * 128 : (j + 1) * 128] for j in range(tiles)], axis=0)
        power = jnp.dot(
            rows, bands, precision=lax.Precision.HIGHEST, preferred_element_type=F32
        ) * F32(1.0 / (2 * BAND))
        inverse = lax.rsqrt(power + F32(1e-06))
        for j in range(tiles):
            inv = inverse[j * 8 : (j + 1) * 8]
            cut = slice(j * 128, (j + 1) * 128)
            both = jnp.concatenate([x0[:, cut] * inv, x1[:, cut] * inv], axis=0).astype(BF16)
            q = max(p for p in range(PARTS) if STARTS[p] <= j * 128)
            o = j * 128 - STARTS[q]
            ws[q][s, :, o : o + 128] = both
        return carry

    lax.fori_loop(0, RING, whiten, 0)
    pl.semaphore_wait(barrier, DEVS - 1)

    def send_ids(slot, peer):
        pltpu.make_async_remote_copy(
            src_ref=meta_ref, dst_ref=ids_all.at[slot],
            send_sem=id_send_sem, recv_sem=id_recv_sem,
            device_id={"sta": peer}, device_id_type=MESH,
        ).start()

    def along_y(i, carry):
        send_ids(inside, row + lax.rem(inside + i, RING))
        return carry

    def along_z(i, carry):
        send_ids(RING + 2 * my_z + my_c, lax.rem(my_z + 1 + i // 2, 4) * RING + 2 * my_y + lax.rem(i, 2))
        return carry

    lax.fori_loop(1, RING, along_y, 0)
    lax.fori_loop(0, 6, along_z, 0)
    ids_all[inside] = meta_ref[...]
    ids_all[RING + 2 * my_z + my_c] = meta_ref[...]

    def send_part(q):
        def one(i, carry):
            peer = lax.rem(me + i * 11, MEMBERS)
            pltpu.make_async_remote_copy(
                src_ref=ws[q].at[slab_of(peer)], dst_ref=wr[q].at[me],
                send_sem=w_send_sem.at[q], recv_sem=w_recv_sem.at[q],
                device_id={"sta": peer}, device_id_type=MESH,
            ).start()
            return carry

        lax.fori_loop(1, MEMBERS, one, 0)
        wr[q][me] = ws[q][my_slab]

    for q in range(PARTS):
        send_part(q)

    start = my_slab * SLAB

    def table_column(cb, half):
        column = lax.broadcasted_iota(jnp.int32, (64, 128), 1) + cb * 128
        cosine_side = column < SIDE
        lags = jnp.where(cosine_side, column, column - SIDE)
        freqs = lax.broadcasted_iota(jnp.int32, (64, 128), 0) + start
        theta = angles(freqs, lags)
        cosines, sines = jnp.cos(theta), jnp.sin(theta)
        turn = angles(jnp.full((8, 128), 64, jnp.int32), lags[:8])
        tc = jnp.concatenate([jnp.cos(turn)] * 8, axis=0)
        ts = jnp.concatenate([jnp.sin(turn)] * 8, axis=0)

        def rotate(i, state):
            c, s = state
            for step in range(4):
                rows = pl.ds(pl.multiple_of(i * 256 + step * 64, 64), 64)
                if half == "both":
                    tcos[rows, SIDE - 64 : SIDE + 64] = jnp.where(cosine_side, c, F32(0)).astype(BF16)
                    tsin[rows, :128] = jnp.where(cosine_side, F32(0), -s).astype(BF16)
                elif half == "cos":
                    tcos[rows, pl.ds(pl.multiple_of(cb * 128, 128), 128)] = c.astype(BF16)
                else:
                    tsin[rows, pl.ds(pl.multiple_of(cb * 128 - 768, 128), 128)] = (-s).astype(BF16)
                c, s = c * tc - s * ts, s * tc + c * ts
            return c, s

        lax.fori_loop(0, SLAB // 256, rotate, (cosines, sines))

    def cosine_column(cb, carry):
        table_column(cb, "cos")
        return carry

    def sine_column(cb, carry):
        table_column(cb, "sin")
        return carry

    lax.fori_loop(0, 6, cosine_column, 0)
    table_column(6, "both")
    lax.fori_loop(7, 13, sine_column, 0)

    known = ids_all.at[pl.ds(0, 13)]
    pltpu.make_async_copy(known, known, id_recv_sem).wait()
    ids_all[RING + 2 * my_z + 1 - my_c] = ids_all[2 * my_y + 1 - my_c]

    def choose(m, carry):
        station = lax.broadcasted_iota(jnp.int32, (STATIONS, 128), 0)
        for line in range(2):
            for side in range(2):
                wanted = ids_all[line * RING + m, side : side + 1, :]
                hot = jnp.transpose(jnp.where(station == wanted, F32(1), F32(0))).astype(BF16)
                for i in range(SHARE // 16):
                    at, pair = i * 32 + side * 16, line * SHARE + i * 16
                    sel[line * RING + m, at : at + 16, :] = hot[pair : pair + 16]
        return carry

    lax.fori_loop(0, RING, choose, 0)

    for q in range(PARTS):
        width = WIDTHS[q]
        arrived = wr[q].at[pl.ds(0, MEMBERS - 1)]
        pltpu.make_async_copy(arrived, arrived, w_recv_sem.at[q]).wait()

        def repack(i, carry):
            both = wr[q][pl.ds(2 * i, 2)].astype(F32)
            rows = pl.ds(pl.multiple_of(i * 16, 16), 16)
            low = both[:, :8].reshape(16, width).astype(BF16)
            high = both[:, 8:].reshape(16, width).astype(BF16)
            for j in range(width // 128):
                wc[j, rows, :128] = low[:, j * 128 : (j + 1) * 128]
                wc[j, rows, 128:] = high[:, j * 128 : (j + 1) * 128]
            return carry

        lax.fori_loop(0, MEMBERS // 2, repack, 0)

        def correlate(j, carry):
            real_at = pl.ds(pl.multiple_of(j * 128, 128), 128)
            imag_at = pl.ds(pl.multiple_of(768 + j * 128, 128), 128)
            for m in range(0, BLOCKS, 8):
                both = jnp.dot(
                    sel[m : m + 8].reshape(8 * 2 * SHARE, STATIONS), wc[j], preferred_element_type=F32
                )
                for i in range(8 * SHARE // 16):
                    a0, a1 = both[i * 32 : i * 32 + 16, :128], both[i * 32 : i * 32 + 16, 128:]
                    b0, b1 = both[i * 32 + 16 : i * 32 + 32, :128], both[i * 32 + 16 : i * 32 + 32, 128:]
                    rows = slice(m * SHARE + i * 16, m * SHARE + i * 16 + 16)
                    cross[rows, real_at] = (a0 * b0 + a1 * b1).astype(BF16)
                    cross[rows, imag_at] = (a1 * b0 - a0 * b1).astype(BF16)
            return carry

        lax.fori_loop(0, width // 128, correlate, 0)

        bins = slice(STARTS[q], STARTS[q] + width)

        def add(columns, value):
            if q == 0:
                acc[:, columns] = value
            else:
                acc[:, columns] += value

        def transform(t, carry):
            left = pl.ds(pl.multiple_of(t * 256, 256), 256)
            right = pl.ds(pl.multiple_of(t * 256 + 128, 128), 256)
            far = pl.ds(pl.multiple_of(t * 256 + 896, 128), 256)
            add(left, jnp.dot(cross[:, :width], tcos[bins, left], preferred_element_type=F32))
            add(far, jnp.dot(cross[:, 768 : 768 + width], tsin[bins, right], preferred_element_type=F32))
            return carry

        lax.fori_loop(0, 3, transform, 0)
        add(
            slice(768, 896),
            jnp.dot(cross[:, :width], tcos[bins, 768:], preferred_element_type=F32)
            + jnp.dot(cross[:, 768 : 768 + width], tsin[bins, :128], preferred_element_type=F32),
        )

    places = (my_y, my_z)

    def block(line, k, c):
        return pl.ds(pl.multiple_of((line * RING + 2 * k + c) * SHARE, 16), SHARE)

    steps = [(i, line) for i in (2, 1, 3, 0) for line in range(2)]
    a_copies = [[], []]
    for p, (first, width) in enumerate(PIECES):
        for n, (i, line) in enumerate(steps):
            k = lax.rem(places[line] + i, 4)
            a_send[p][n] = acc[block(line, k, 1 - my_c), first : first + width].astype(BF16)
            copy = pltpu.make_async_remote_copy(
                src_ref=a_send[p].at[n], dst_ref=a_recv[p].at[n],
                send_sem=a_send_sem.at[p, n], recv_sem=a_recv_sem.at[p, n],
                device_id={"sta": me + 1 - 2 * my_c}, device_id_type=MESH,
            )
            copy.start()
            a_copies[p].append(copy)

    b_copies = [[], []]
    for p, (first, width) in enumerate(PIECES):
        for n, (i, line) in enumerate(steps[:6]):
            k = lax.rem(places[line] + i, 4)
            a_copies[p][n].wait_recv()
            mine = acc[block(line, k, my_c), first : first + width]
            b_send[p][n] = (mine + a_recv[p][n].astype(F32)).astype(BF16)
            peer = row + 2 * k + my_c if line == 0 else k * RING + inside
            copy = pltpu.make_async_remote_copy(
                src_ref=b_send[p].at[n], dst_ref=b_recv[p].at[n],
                send_sem=b_send_sem.at[p, n], recv_sem=b_recv_sem.at[p, n],
                device_id={"sta": peer}, device_id_type=MESH,
            )
            copy.start()
            b_copies[p].append(copy)

    meta = meta_ref[...]
    square = (128, 128)
    sub, lane = lax.broadcasted_iota(jnp.int32, square, 0), lax.broadcasted_iota(jnp.int32, square, 1)
    dest = meta[3:4, :]
    dest_across = jnp.transpose(jnp.broadcast_to(dest.astype(F32), square)).astype(jnp.int32)
    earlier = (dest_across == dest) & (sub < lane) & (sub < PAIRS)
    position = jnp.sum(jnp.where(earlier, F32(1), F32(0)), axis=0, keepdims=True).astype(jnp.int32)
    counted = (lane[0:1] < PAIRS) & (meta[2:3, :] == 1)
    code = jnp.where(counted, dest * 8 + position * SEGS, -64)

    def place(t, carry):
        target = lax.broadcasted_iota(jnp.int32, (128, 128), 0) + t * 128
        rows = pl.ds(pl.multiple_of(t * 128, 128), 128)
        for k in range(SEGS):
            gsel[rows, k * 128 : (k + 1) * 128] = jnp.where(target == code + k, F32(1), F32(0)).astype(BF16)
        return carry

    lax.fori_loop(0, DEVS * 8 // 128, place, 0)
    slot_across = jnp.transpose(jnp.broadcast_to(meta[4:5, :].astype(F32), square)).astype(BF16)
    for p in range(2):
        corr[p][...] = jnp.zeros_like(corr[p])
    corr[1][3 * 128 :, :128] = slot_across
    corr[1][3 * 128 :, 128:] = slot_across

    scale = F32(BINS ** (-0.5))
    owns = []
    for p, (first, width) in enumerate(PIECES):
        for line in range(2):
            a_copies[p][6 + line].wait_recv()
            for n in range(line, 6, 2):
                b_copies[p][n].wait_recv()
            total = acc[block(line, places[line], my_c), first : first + width]
            total = total + a_recv[p][6 + line].astype(F32)
            for n in range(line, 6, 2):
                total = total + b_recv[p][n].astype(F32)
            total = (total * scale).astype(BF16)
            for k in range(-(-width // SEG)):
                wide = min(SEG, width - k * SEG)
                at = k * 128 + line * SHARE
                corr[p][at : at + SHARE, :wide] = total[:, k * SEG : k * SEG + wide]

        def pack(t, carry):
            rows = pl.ds(pl.multiple_of(t * 256, 256), 256)
            out = jnp.dot(gsel[rows, :], corr[p][...], preferred_element_type=F32)
            c_send[p][pl.ds(t * 32, 32)] = out.reshape(32, 8, SEG).astype(BF16)
            return carry

        lax.fori_loop(0, DEVS // 32, pack, 0)
        own = pltpu.make_async_copy(c_send[p].at[dev], got[p].at[dev], own_sem.at[p])
        own.start()
        owns.append(own)

        def route(i, carry):
            peer = lax.rem(dev + i * 53, DEVS)
            pltpu.make_async_remote_copy(
                src_ref=c_send[p].at[peer], dst_ref=got[p].at[dev],
                send_sem=c_send_sem.at[p], recv_sem=c_recv_sem.at[p],
                device_id={"grp": peer // MEMBERS, "sta": lax.rem(peer, MEMBERS)},
                device_id_type=MESH,
            ).start()
            return carry

        lax.fori_loop(1, DEVS, route, 0)

    for p in range(2):
        for copy in a_copies[p]:
            copy.wait_send()
        for copy in b_copies[p]:
            copy.wait_send()
    pltpu.make_async_copy(known, known, id_send_sem).wait()
    for q in range(PARTS):
        sent = wr[q].at[pl.ds(0, MEMBERS - 1)]
        pltpu.make_async_copy(sent, sent, w_send_sem.at[q]).wait()
    for p in range(2):
        owns[p].wait()
        rest = c_send[p].at[pl.ds(0, DEVS - 1)]
        pltpu.make_async_copy(rest, rest, c_send_sem.at[p]).wait()
        pltpu.make_async_copy(rest, rest, c_recv_sem.at[p]).wait()


def correlate_and_route(x, meta):
    vmem = pl.BlockSpec(memory_space=pltpu.VMEM)
    dma = pltpu.SemaphoreType.DMA
    return pl.pallas_call(
        main_kernel,
        out_shape=[jax.ShapeDtypeStruct((DEVS, 8, SEG), BF16)] * 2,
        in_specs=[vmem] * 2,
        out_specs=[pl.BlockSpec(memory_space=pl.ANY)] * 2,
        scratch_shapes=[
            *[pltpu.VMEM((RING, 16, w), BF16) for w in WIDTHS],
            *[pltpu.VMEM((MEMBERS, 16, w), BF16) for w in WIDTHS],
            pltpu.VMEM((max(WIDTHS) // 128, STATIONS, 256), BF16),
            pltpu.VMEM((BLOCKS, 8, 128), jnp.int32),
            pltpu.VMEM((BLOCKS, 2 * SHARE, STATIONS), BF16),
            pltpu.VMEM((SLAB, 896), BF16),
            pltpu.VMEM((SLAB, 896), BF16),
            pltpu.VMEM((RING * PAIRS, COLS), F32),
            pltpu.VMEM((RING * PAIRS, 2 * max(WIDTHS)), BF16),
            *[pltpu.VMEM((8, SHARE, w), BF16) for _ in range(2) for _, w in PIECES],
            *[pltpu.VMEM((6, SHARE, w), BF16) for _ in range(2) for _, w in PIECES],
            *[pltpu.VMEM((SEGS * 128, SEG), BF16) for _ in range(2)],
            pltpu.VMEM((DEVS * 8, SEGS * 128), BF16),
            *[pltpu.VMEM((DEVS, 8, SEG), BF16) for _ in range(2)],
            dma, dma,
            dma((PARTS,)), dma((PARTS,)),
            dma((2, 8)), dma((2, 8)),
            dma((2, 6)), dma((2, 6)),
            dma((2,)), dma((2,)), dma((2,)),
        ],
        compiler_params=pltpu.CompilerParams(
            collective_id=0, has_side_effects=True, vmem_limit_bytes=46 * 1024 * 1024
        ),
    )(x, meta)


def stack_kernel(got_a, got_b, stacks_ref, out_ref):
    rows = DEVS * 8
    got = [ref[...].reshape(rows, SEG) for ref in (got_a, got_b)]
    first = jnp.where(lax.broadcasted_iota(jnp.int32, (8, SEG), 1) == 0, F32(1), F32(0)).astype(BF16)
    marks = lax.dot_general(first, got[1], (((1,), (1,)), ((), ())), preferred_element_type=F32)
    place = lax.broadcasted_iota(jnp.int32, (8, rows), 1) & 3
    marks = jnp.where(place == 3, marks, F32(0))
    marks = jnp.maximum(marks, pltpu.roll(marks, rows - 1, 1))
    marks = jnp.maximum(marks, pltpu.roll(marks, rows - 2, 1))
    code = (marks.astype(jnp.int32) + place * PAIRS)[0:1]
    parts = [[], []]
    for k in range(SEGS):
        want = lax.broadcasted_iota(jnp.int32, (PAIRS, rows), 0) + k * PAIRS
        hot = jnp.where(want == code, F32(1), F32(0)).astype(BF16)
        for p in range(2 if k < 3 else 1):
            parts[p].append(jnp.dot(hot, got[p], preferred_element_type=F32))
    parts = parts[0] + parts[1]
    sums = jnp.concatenate(parts, axis=1)
    even, odd = sums[:, :896], sums[:, SIDE : SIDE + 896]
    tiles = 7
    gap = even - odd
    high = gap.astype(BF16)
    low = (gap - high.astype(F32)).astype(BF16)
    stack = jnp.concatenate(
        [v[:, t * 128 : (t + 1) * 128] for v in (high, low) for t in range(tiles)], axis=0
    )
    mirror = lax.broadcasted_iota(jnp.int32, (128, 128), 0) + lax.broadcasted_iota(jnp.int32, (128, 128), 1)
    mirror = jnp.where(mirror == 127, F32(1), F32(0)).astype(BF16)
    turned = jnp.dot(stack, mirror, preferred_element_type=F32)
    turned = turned[: tiles * PAIRS] + turned[tiles * PAIRS :]
    behind = jnp.concatenate(
        [turned[t * PAIRS : (t + 1) * PAIRS] for t in reversed(range(tiles))], axis=1
    )
    skip = tiles * 128 - HALF
    out_ref[:, :HALF] = stacks_ref[:, :HALF] + behind[:, skip:]
    out_ref[:, HALF:] = stacks_ref[:, HALF:] + (even + odd)[:, 1:HALF]


def add_rows(got_a, got_b, stacks):
    vmem = pl.BlockSpec(memory_space=pltpu.VMEM)
    return pl.pallas_call(
        stack_kernel,
        out_shape=jax.ShapeDtypeStruct(stacks.shape, F32),
        in_specs=[vmem] * 3,
        out_specs=vmem,
        compiler_params=pltpu.CompilerParams(vmem_limit_bytes=40 * 1024 * 1024),
    )(got_a, got_b, stacks)


def local(spectra, stacks, pair_sta, pair_valid, owner, slot):
    rows = [pair_sta, pair_valid[None, :], owner.reshape(1, PAIRS), slot[None, :]]
    meta = jnp.pad(jnp.concatenate(rows, axis=0), ((0, 3), (0, 128 - PAIRS)))
    got_a, got_b = correlate_and_route(spectra, meta)
    return add_rows(got_a, got_b, stacks)


def solution(mesh):
    return jax.shard_map(
        local,
        mesh=mesh,
        in_specs=(
            P(("grp", "sta"), None, None),
            P(("grp", "sta"), None),
            P(None, ("grp", "sta")),
            P(("grp", "sta")),
            P(("grp", "sta"), None),
            P(("grp", "sta")),
        ),
        out_specs=P(("grp", "sta"), None),
        check_vma=False,
    )
```

time: 86.5 us -> 75 us (0.87)
  Pallas kernels: 84.3 us -> 72.8 us
    pallas_call x1, Pallas kernels: 81.2 us -> 70.4 us  [correlate_and_route(): pl.pallas_call(main_kernel, out_shape=[jax.ShapeDtypeStruct((DEVS, 8, SEG...]
where the time goes in v3:
time: 75 us; the launch traced here: 74.8 us
  Pallas kernels  72.8 us (97%)
  local copies, waits for them, and re-layouts  1.27 us (2%)
    pallas_call x1, Pallas kernels, correlate_and_route(): pl.pallas_call(main_kernel, out_shape=[jax.ShapeDtypeStruct((DEVS, 8, SEG...  70.4 us
    pallas_call x1, Pallas kernels, add_rows(): pl.pallas_call(stack_kernel, out_shape=jax.ShapeDtypeStruct(stacks.shape,...  2.35 us

profile of v3, /device:TPU:1, one launch (start us, length us, event | category | flops | bytes accessed | tf_op | source)
XLA Modules:
  0.0 74.8 jit_solution(16371479497739237717)
XLA Ops:
  0.0 0.7 pad_add_fusion
  0.7 0.0 copy-start
  0.8 1.3 %copy-done = f32[8,2,18432]{2,1,0:T(2,128)S(1)} copy-done((f32[8,2,18432]{2,1,0:T(2,128)S(1)}, f32[8,2,18432]{2,1,0:T(2,128)}, u32[]{:S(2)}) %copy-start) | copy-done | bytes 1179672
  2.0 0.0 copy-start.1
  2.0 70.4 %shard_map.64 = (bf16[128,8,256]{2,1,0:T(8,128)(2,1)S(1)}, bf16[128,8,256]{2,1,0:T(8,128)(2,1)S(1)}) custom-call(f32[8,2,18432]{2,1,0:T(2,128)S(1)} %copy-done, s32[8,128]{1,0:T(8,128)S(1)} %pad.4.meta_ref), custom_call_target="tpu_custom_call" | custom-call | tf_op jit(solution)/shard_map/pallas_call | solution.py:378
  72.4 0.0 copy-done.1
  72.5 2.3 %shard_map.65 = f32[96,1601]{1,0:T(8,128)} custom-call(bf16[128,8,256]{2,1,0:T(8,128)(2,1)S(1)} %get-tuple-element.7.got_a, bf16[128,8,256]{2,1,0:T(8,128)(2,1)S(1)} %get-tuple-element.8.got_b, f32[96,1601]{1,0:T(8,128)S(1)} %copy-done.1), custom_call_target="tpu_custom_call" | custom-call | tf_op jit(solution)/shard_map/pallas_call | solution.py:450
  (1 shorter events, 0.0 us)
Async XLA Ops:
  0.7 1.3 %copy-start = (f32[8,2,18432]{2,1,0:T(2,128)S(1)}, f32[8,2,18432]{2,1,0:T(2,128)}, u32[]{:S(2)}) copy-start(f32[8,2,18432]{2,1,0:T(2,128)} %x_ref.1) | copy-start | bytes 3538948
  2.0 70.4 %copy-start.1 = (f32[96,1601]{1,0:T(8,128)S(1)}, f32[96,1601]{1,0:T(8,128)}, u32[]{:S(2)}) copy-start(f32[96,1601]{1,0:T(8,128)} %stacks_ref.1) | copy-start | bytes 1844356

commit v4 on v3

--- a/solution.py
+++ b/solution.py
@@ -23,8 +23,9 @@
 RING = 8
 BLOCKS = 2 * RING
 SLAB = BINS // RING
-WIDTHS = (768, 768, 512, 256)
-STARTS = (0, 768, 1536, 2048)
+WIDTHS = (512, 512, 512, 512, 256)
+STARTS = (0, 512, 1024, 1536, 2048)
+WIDE = max(WIDTHS)
 PARTS = len(WIDTHS)
 MEMBERS = 32
 GROUPS = 4
@@ -32,7 +33,7 @@
 STATIONS = 256
 SEG = 256
 SEGS = 4
-PIECES = ((0, 1024), (1024, 640))
+PIECES = ((1024, 640), (0, 1024))
 
 
 def angles(freqs, shifts):
@@ -41,14 +42,14 @@
     return (product - turns * F32(2 * BINS)) * F32(math.pi / BINS)
 
 
-def main_kernel(x_ref, meta_ref, got_a, got_b, *scratch):
+def main_kernel(spectra_ref, pair_ref, valid_ref, owner_ref, slot_ref, got_a, got_b, *scratch):
     ws, wr = scratch[:PARTS], scratch[PARTS : 2 * PARTS]
     (
-        wc, ids_all, sel, tcos, tsin, acc, cross,
+        x_ref, meta_ref, wc, ids_all, sel, tcos, tsin, acc, cross,
         a_send_0, a_send_1, a_recv_0, a_recv_1, b_send_0, b_send_1, b_recv_0, b_recv_1,
         corr_0, corr_1, gsel, c_send_0, c_send_1,
         id_send_sem, id_recv_sem, w_send_sem, w_recv_sem,
-        a_send_sem, a_recv_sem, b_send_sem, b_recv_sem, c_send_sem, c_recv_sem, own_sem,
+        a_send_sem, a_recv_sem, b_send_sem, b_recv_sem, c_send_sem, c_recv_sem, own_sem, x_sem,
     ) = scratch[2 * PARTS :]
     a_send, a_recv = (a_send_0, a_send_1), (a_recv_0, a_recv_1)
     b_send, b_recv = (b_send_0, b_send_1), (b_recv_0, b_recv_1)
@@ -66,6 +67,13 @@
     my_slab = slab_of(me)
     row = me - inside
 
+    def load(s):
+        bins = pl.ds(pl.multiple_of(s * SLAB, 128), SLAB)
+        return pltpu.make_async_copy(spectra_ref.at[:, :, bins], x_ref.at[:, :, bins], x_sem.at[s])
+
+    for s in range(RING):
+        load(s).start()
+
     barrier = pltpu.get_barrier_semaphore()
 
     def greet(i, carry):
@@ -79,11 +87,18 @@
 
     lax.fori_loop(1, DEVS, greet, 0)
 
+    meta_ref[...] = jnp.zeros_like(meta_ref)
+    meta_ref[0:2, :PAIRS] = pair_ref[...]
+    meta_ref[2:3, :PAIRS] = valid_ref[...]
+    meta_ref[3:4, :PAIRS] = owner_ref[...]
+    meta_ref[4:5, :PAIRS] = slot_ref[...]
+
     lane = lax.broadcasted_iota(jnp.int32, (128, 128), 1) // BAND
     sub = lax.broadcasted_iota(jnp.int32, (128, 128), 0) // BAND
     bands = jnp.where(lane == sub, F32(1), F32(0))
 
     def whiten(s, carry):
+        load(s).wait()
         base = pl.multiple_of(s * SLAB, 128)
         x0 = x_ref[:, 0, pl.ds(base, SLAB)]
         x1 = x_ref[:, 1, pl.ds(base, SLAB)]
@@ -200,62 +215,29 @@
 
     lax.fori_loop(0, RING, choose, 0)
 
-    for q in range(PARTS):
-        width = WIDTHS[q]
-        arrived = wr[q].at[pl.ds(0, MEMBERS - 1)]
-        pltpu.make_async_copy(arrived, arrived, w_recv_sem.at[q]).wait()
-
-        def repack(i, carry):
-            both = wr[q][pl.ds(2 * i, 2)].astype(F32)
-            rows = pl.ds(pl.multiple_of(i * 16, 16), 16)
-            low = both[:, :8].reshape(16, width).astype(BF16)
-            high = both[:, 8:].reshape(16, width).astype(BF16)
-            for j in range(width // 128):
-                wc[j, rows, :128] = low[:, j * 128 : (j + 1) * 128]
-                wc[j, rows, 128:] = high[:, j * 128 : (j + 1) * 128]
-            return carry
-
-        lax.fori_loop(0, MEMBERS // 2, repack, 0)
-
-        def correlate(j, carry):
-            real_at = pl.ds(pl.multiple_of(j * 128, 128), 128)
-            imag_at = pl.ds(pl.multiple_of(768 + j * 128, 128), 128)
-            for m in range(0, BLOCKS, 8):
-                both = jnp.dot(
-                    sel[m : m + 8].reshape(8 * 2 * SHARE, STATIONS), wc[j], preferred_element_type=F32
-                )
-                for i in range(8 * SHARE // 16):
-                    a0, a1 = both[i * 32 : i * 32 + 16, :128], both[i * 32 : i * 32 + 16, 128:]
-                    b0, b1 = both[i * 32 + 16 : i * 32 + 32, :128], both[i * 32 + 16 : i * 32 + 32, 128:]
-                    rows = slice(m * SHARE + i * 16, m * SHARE + i * 16 + 16)
-                    cross[rows, real_at] = (a0 * b0 + a1 * b1).astype(BF16)
-                    cross[rows, imag_at] = (a1 * b0 - a0 * b1).astype(BF16)
-            return carry
-
-        lax.fori_loop(0, width // 128, correlate, 0)
-
-        bins = slice(STARTS[q], STARTS[q] + width)
-
-        def add(columns, value):
-            if q == 0:
-                acc[:, columns] = value
-            else:
-                acc[:, columns] += value
-
-        def transform(t, carry):
-            left = pl.ds(pl.multiple_of(t * 256, 256), 256)
-            right = pl.ds(pl.multiple_of(t * 256 + 128, 128), 256)
-            far = pl.ds(pl.multiple_of(t * 256 + 896, 128), 256)
-            add(left, jnp.dot(cross[:, :width], tcos[bins, left], preferred_element_type=F32))
-            add(far, jnp.dot(cross[:, 768 : 768 + width], tsin[bins, right], preferred_element_type=F32))
-            return carry
-
-        lax.fori_loop(0, 3, transform, 0)
-        add(
-            slice(768, 896),
-            jnp.dot(cross[:, :width], tcos[bins, 768:], preferred_element_type=F32)
-            + jnp.dot(cross[:, 768 : 768 + width], tsin[bins, :128], preferred_element_type=F32),
-        )
+    meta = meta_ref[...]
+    square = (128, 128)
+    sub, lane = lax.broadcasted_iota(jnp.int32, square, 0), lax.broadcasted_iota(jnp.int32, square, 1)
+    dest = meta[3:4, :]
+    dest_across = jnp.transpose(jnp.broadcast_to(dest.astype(F32), square)).astype(jnp.int32)
+    earlier = (dest_across == dest) & (sub < lane) & (sub < PAIRS)
+    position = jnp.sum(jnp.where(earlier, F32(1), F32(0)), axis=0, keepdims=True).astype(jnp.int32)
+    counted = (lane[0:1] < PAIRS) & (meta[2:3, :] == 1)
+    code = jnp.where(counted, dest * 8 + position * SEGS, -64)
+
+    def place(t, carry):
+        target = lax.broadcasted_iota(jnp.int32, (128, 128), 0) + t * 128
+        rows = pl.ds(pl.multiple_of(t * 128, 128), 128)
+        for k in range(SEGS):
+            gsel[rows, k * 128 : (k + 1) * 128] = jnp.where(target == code + k, F32(1), F32(0)).astype(BF16)
+        return carry
+
+    lax.fori_loop(0, DEVS * 8 // 128, place, 0)
+    slot_across = jnp.transpose(jnp.broadcast_to(meta[4:5, :].astype(F32), square)).astype(BF16)
+    for p in range(2):
+        corr[p][...] = jnp.zeros_like(corr[p])
+    corr[0][3 * 128 :, :128] = slot_across
+    corr[0][3 * 128 :, 128:] = slot_across
 
     places = (my_y, my_z)
 
@@ -264,7 +246,9 @@
 
     steps = [(i, line) for i in (2, 1, 3, 0) for line in range(2)]
     a_copies = [[], []]
-    for p, (first, width) in enumerate(PIECES):
+
+    def send_a(p):
+        first, width = PIECES[p]
         for n, (i, line) in enumerate(steps):
             k = lax.rem(places[line] + i, 4)
             a_send[p][n] = acc[block(line, k, 1 - my_c), first : first + width].astype(BF16)
@@ -275,6 +259,62 @@
             )
             copy.start()
             a_copies[p].append(copy)
+
+    for q in range(PARTS):
+        width = WIDTHS[q]
+        arrived = wr[q].at[pl.ds(0, MEMBERS - 1)]
+        pltpu.make_async_copy(arrived, arrived, w_recv_sem.at[q]).wait()
+
+        def repack(i, carry):
+            both = wr[q][pl.ds(2 * i, 2)].astype(F32)
+            rows = pl.ds(pl.multiple_of(i * 16, 16), 16)
+            low = both[:, :8].reshape(16, width).astype(BF16)
+            high = both[:, 8:].reshape(16, width).astype(BF16)
+            for j in range(width // 128):
+                wc[j, rows, :128] = low[:, j * 128 : (j + 1) * 128]
+                wc[j, rows, 128:] = high[:, j * 128 : (j + 1) * 128]
+            return carry
+
+        lax.fori_loop(0, MEMBERS // 2, repack, 0)
+
+        def correlate(pair, carry):
+            for j in (2 * pair, 2 * pair + 1):
+                real_at = pl.ds(pl.multiple_of(j * 128, 128), 128)
+                imag_at = pl.ds(pl.multiple_of(WIDE + j * 128, 128), 128)
+                for m in range(0, BLOCKS, 8):
+                    both = jnp.dot(
+                        sel[m : m + 8].reshape(8 * 2 * SHARE, STATIONS), wc[j], preferred_element_type=F32
+                    )
+                    for i in range(8 * SHARE // 16):
+                        a0, a1 = both[i * 32 : i * 32 + 16, :128], both[i * 32 : i * 32 + 16, 128:]
+                        b0, b1 = both[i * 32 + 16 : i * 32 + 32, :128], both[i * 32 + 16 : i * 32 + 32, 128:]
+                        rows = slice(m * SHARE + i * 16, m * SHARE + i * 16 + 16)
+                        cross[rows, real_at] = (a0 * b0 + a1 * b1).astype(BF16)
+                        cross[rows, imag_at] = (a1 * b0 - a0 * b1).astype(BF16)
+            return carry
+
+        lax.fori_loop(0, width // 256, correlate, 0)
+
+        bins = slice(STARTS[q], STARTS[q] + width)
+
+        def add(columns, value):
+            if q == 0:
+                acc[:, columns] = value
+            else:
+                acc[:, columns] += value
+
+        real, imag = cross.at[:, :width], cross.at[:, WIDE : WIDE + width]
+        add(slice(896, COLS), jnp.dot(imag[...], tsin[bins, 128:], preferred_element_type=F32))
+        if q == PARTS - 1:
+            send_a(0)
+        add(slice(0, 768), jnp.dot(real[...], tcos[bins, :768], preferred_element_type=F32))
+        add(
+            slice(768, 896),
+            jnp.dot(real[...], tcos[bins, 768:], preferred_element_type=F32)
+            + jnp.dot(imag[...], tsin[bins, :128], preferred_element_type=F32),
+        )
+        if q == PARTS - 1:
+            send_a(1)
 
     b_copies = [[], []]
     for p, (first, width) in enumerate(PIECES):
@@ -291,30 +331,6 @@
             )
             copy.start()
             b_copies[p].append(copy)
-
-    meta = meta_ref[...]
-    square = (128, 128)
-    sub, lane = lax.broadcasted_iota(jnp.int32, square, 0), lax.broadcasted_iota(jnp.int32, square, 1)
-    dest = meta[3:4, :]
-    dest_across = jnp.transpose(jnp.broadcast_to(dest.astype(F32), square)).astype(jnp.int32)
-    earlier = (dest_across == dest) & (sub < lane) & (sub < PAIRS)
-    position = jnp.sum(jnp.where(earlier, F32(1), F32(0)), axis=0, keepdims=True).astype(jnp.int32)
-    counted = (lane[0:1] < PAIRS) & (meta[2:3, :] == 1)
-    code = jnp.where(counted, dest * 8 + position * SEGS, -64)
-
-    def place(t, carry):
-        target = lax.broadcasted_iota(jnp.int32, (128, 128), 0) + t * 128
-        rows = pl.ds(pl.multiple_of(t * 128, 128), 128)
-        for k in range(SEGS):
-            gsel[rows, k * 128 : (k + 1) * 128] = jnp.where(target == code + k, F32(1), F32(0)).astype(BF16)
-        return carry
-
-    lax.fori_loop(0, DEVS * 8 // 128, place, 0)
-    slot_across = jnp.transpose(jnp.broadcast_to(meta[4:5, :].astype(F32), square)).astype(BF16)
-    for p in range(2):
-        corr[p][...] = jnp.zeros_like(corr[p])
-    corr[1][3 * 128 :, :128] = slot_across
-    corr[1][3 * 128 :, 128:] = slot_across
 
     scale = F32(BINS ** (-0.5))
     owns = []
@@ -372,24 +388,26 @@
         pltpu.make_async_copy(rest, rest, c_recv_sem.at[p]).wait()
 
 
-def correlate_and_route(x, meta):
+def correlate_and_route(*operands):
     vmem = pl.BlockSpec(memory_space=pltpu.VMEM)
     dma = pltpu.SemaphoreType.DMA
     return pl.pallas_call(
         main_kernel,
         out_shape=[jax.ShapeDtypeStruct((DEVS, 8, SEG), BF16)] * 2,
-        in_specs=[vmem] * 2,
+        in_specs=[pl.BlockSpec(memory_space=pltpu.HBM)] + [vmem] * 4,
         out_specs=[pl.BlockSpec(memory_space=pl.ANY)] * 2,
         scratch_shapes=[
             *[pltpu.VMEM((RING, 16, w), BF16) for w in WIDTHS],
             *[pltpu.VMEM((MEMBERS, 16, w), BF16) for w in WIDTHS],
-            pltpu.VMEM((max(WIDTHS) // 128, STATIONS, 256), BF16),
+            pltpu.VMEM((RING, 2, BINS), F32),
+            pltpu.VMEM((8, 128), jnp.int32),
+            pltpu.VMEM((WIDE // 128, STATIONS, 256), BF16),
             pltpu.VMEM((BLOCKS, 8, 128), jnp.int32),
             pltpu.VMEM((BLOCKS, 2 * SHARE, STATIONS), BF16),
             pltpu.VMEM((SLAB, 896), BF16),
             pltpu.VMEM((SLAB, 896), BF16),
             pltpu.VMEM((RING * PAIRS, COLS), F32),
-            pltpu.VMEM((RING * PAIRS, 2 * max(WIDTHS)), BF16),
+            pltpu.VMEM((RING * PAIRS, 2 * WIDE), BF16),
             *[pltpu.VMEM((8, SHARE, w), BF16) for _ in range(2) for _, w in PIECES],
             *[pltpu.VMEM((6, SHARE, w), BF16) for _ in range(2) for _, w in PIECES],
             *[pltpu.VMEM((SEGS * 128, SEG), BF16) for _ in range(2)],
@@ -399,19 +417,19 @@
             dma((PARTS,)), dma((PARTS,)),
             dma((2, 8)), dma((2, 8)),
             dma((2, 6)), dma((2, 6)),
-            dma((2,)), dma((2,)), dma((2,)),
+            dma((2,)), dma((2,)), dma((2,)), dma((RING,)),
         ],
         compiler_params=pltpu.CompilerParams(
             collective_id=0, has_side_effects=True, vmem_limit_bytes=46 * 1024 * 1024
         ),
-    )(x, meta)
+    )(*operands)
 
 
 def stack_kernel(got_a, got_b, stacks_ref, out_ref):
     rows = DEVS * 8
     got = [ref[...].reshape(rows, SEG) for ref in (got_a, got_b)]
     first = jnp.where(lax.broadcasted_iota(jnp.int32, (8, SEG), 1) == 0, F32(1), F32(0)).astype(BF16)
-    marks = lax.dot_general(first, got[1], (((1,), (1,)), ((), ())), preferred_element_type=F32)
+    marks = lax.dot_general(first, got[0], (((1,), (1,)), ((), ())), preferred_element_type=F32)
     place = lax.broadcasted_iota(jnp.int32, (8, rows), 1) & 3
     marks = jnp.where(place == 3, marks, F32(0))
     marks = jnp.maximum(marks, pltpu.roll(marks, rows - 1, 1))
@@ -421,9 +439,9 @@
     for k in range(SEGS):
         want = lax.broadcasted_iota(jnp.int32, (PAIRS, rows), 0) + k * PAIRS
         hot = jnp.where(want == code, F32(1), F32(0)).astype(BF16)
-        for p in range(2 if k < 3 else 1):
+        for p in range(0 if k < 3 else 1, 2):
             parts[p].append(jnp.dot(hot, got[p], preferred_element_type=F32))
-    parts = parts[0] + parts[1]
+    parts = parts[1] + parts[0]
     sums = jnp.concatenate(parts, axis=1)
     even, odd = sums[:, :896], sums[:, SIDE : SIDE + 896]
     tiles = 7
@@ -457,9 +475,9 @@
 
 
 def local(spectra, stacks, pair_sta, pair_valid, owner, slot):
-    rows = [pair_sta, pair_valid[None, :], owner.reshape(1, PAIRS), slot[None, :]]
-    meta = jnp.pad(jnp.concatenate(rows, axis=0), ((0, 3), (0, 128 - PAIRS)))
-    got_a, got_b = correlate_and_route(spectra, meta)
+    got_a, got_b = correlate_and_route(
+        spectra, pair_sta, pair_valid[None, :], owner.reshape(1, PAIRS), slot[None, :]
+    )
     return add_rows(got_a, got_b, stacks)
 
 

time: 75 us -> 73 us (0.973)
  Pallas kernels: 72.8 us -> 68.9 us
  local copies, waits for them, and re-layouts: 1.27 us -> 3.92 us
    pallas_call x1, Pallas kernels: 70.4 us -> 66.6 us  [correlate_and_route(): pl.pallas_call(main_kernel, out_shape=[jax.ShapeDtypeStruct((DEVS, 8, SEG...]
    unnamed x4 -> x12, local copies, waits for them, and re-layouts: 1.27 us -> 3.92 us
where the time goes in v4:
time: 73 us; the launch traced here: 72.8 us
  Pallas kernels  68.9 us (94%)
  local copies, waits for them, and re-layouts  3.92 us (5%)
    pallas_call x1, Pallas kernels, correlate_and_route(): pl.pallas_call(main_kernel, out_shape=[jax.ShapeDtypeStruct((DEVS, 8, SEG...  66.6 us
    unnamed x12, local copies, waits for them, and re-layouts  3.92 us
    pallas_call x1, Pallas kernels, add_rows(): pl.pallas_call(stack_kernel, out_shape=jax.ShapeDtypeStruct(stacks.shape,...  2.35 us

profile of v4, /device:TPU:1, one launch (start us, length us, event | category | flops | bytes accessed | tf_op | source)
XLA Modules:
  0.0 72.8 jit_solution(16898527964063031258)
XLA Ops:
  0.0 0.0 copy-start
  0.0 1.3 %copy-done = f32[8,2,18432]{2,1,0:T(2,128)S(1)} copy-done((f32[8,2,18432]{2,1,0:T(2,128)S(1)}, f32[8,2,18432]{2,1,0:T(2,128)}, u32[]{:S(2)}) %copy-start) | copy-done | bytes 1179672
  1.3 0.0 copy-start.2
  1.3 0.7 copy-done.2
  2.0 0.0 copy-start.3
  2.0 0.7 copy-done.3
  2.6 0.0 copy-start.4
  2.6 0.7 copy-done.4
  3.3 0.0 copy-start.5
  3.3 0.7 copy-done.5
  3.9 0.0 copy-start.1
  3.9 66.6 %shard_map.64 = (bf16[128,8,256]{2,1,0:T(8,128)(2,1)S(1)}, bf16[128,8,256]{2,1,0:T(8,128)(2,1)S(1)}) custom-call(f32[8,2,18432]{2,1,0:T(2,128)S(1)} %copy-done, s32[2,96]{1,0:T(2,128)S(1)} %copy-done.2, s32[1,96]{1,0:T(1,128)S(1)} %bitcast.3, s32[1,96]{1,0:T(1,128)S(1)} %bitcast.4, s32[1,96]{1,0:T(1,128)S(1)} %bitcast.5), custom_call_target="tpu_custom_call" | custom-call | tf_op jit(solution)/shard_map/pallas_call | solution.py:394
  70.5 0.0 copy-done.1
  70.5 2.3 %shard_map.65 = f32[96,1601]{1,0:T(8,128)} custom-call(bf16[128,8,256]{2,1,0:T(8,128)(2,1)S(1)} %get-tuple-element.7.got_a, bf16[128,8,256]{2,1,0:T(8,128)(2,1)S(1)} %get-tuple-element.8.got_b, f32[96,1601]{1,0:T(8,128)S(1)} %copy-done.1), custom_call_target="tpu_custom_call" | custom-call | tf_op jit(solution)/shard_map/pallas_call | solution.py:468
Async XLA Ops:
  0.0 1.3 %copy-start = (f32[8,2,18432]{2,1,0:T(2,128)S(1)}, f32[8,2,18432]{2,1,0:T(2,128)}, u32[]{:S(2)}) copy-start(f32[8,2,18432]{2,1,0:T(2,128)} %spectra_ref.1) | copy-start | bytes 3538948
  1.3 0.7 copy-start.2
  2.0 0.7 copy-start.3
  2.6 0.7 copy-start.4
  3.3 0.7 copy-start.5
  3.9 66.6 %copy-start.1 = (f32[96,1601]{1,0:T(8,128)S(1)}, f32[96,1601]{1,0:T(8,128)}, u32[]{:S(2)}) copy-start(f32[96,1601]{1,0:T(8,128)} %stacks_ref.1) | copy-start | bytes 1844356

commit v5 on v4

--- a/solution.py
+++ b/solution.py
@@ -42,10 +42,10 @@
     return (product - turns * F32(2 * BINS)) * F32(math.pi / BINS)
 
 
-def main_kernel(spectra_ref, pair_ref, valid_ref, owner_ref, slot_ref, got_a, got_b, *scratch):
+def main_kernel(spectra_ref, meta_ref, got_a, got_b, *scratch):
     ws, wr = scratch[:PARTS], scratch[PARTS : 2 * PARTS]
     (
-        x_ref, meta_ref, wc, ids_all, sel, tcos, tsin, acc, cross,
+        x_ref, wc, ids_all, sel, tcos, tsin, acc, cross,
         a_send_0, a_send_1, a_recv_0, a_recv_1, b_send_0, b_send_1, b_recv_0, b_recv_1,
         corr_0, corr_1, gsel, c_send_0, c_send_1,
         id_send_sem, id_recv_sem, w_send_sem, w_recv_sem,
@@ -86,12 +86,6 @@
         return carry
 
     lax.fori_loop(1, DEVS, greet, 0)
-
-    meta_ref[...] = jnp.zeros_like(meta_ref)
-    meta_ref[0:2, :PAIRS] = pair_ref[...]
-    meta_ref[2:3, :PAIRS] = valid_ref[...]
-    meta_ref[3:4, :PAIRS] = owner_ref[...]
-    meta_ref[4:5, :PAIRS] = slot_ref[...]
 
     lane = lax.broadcasted_iota(jnp.int32, (128, 128), 1) // BAND
     sub = lax.broadcasted_iota(jnp.int32, (128, 128), 0) // BAND
@@ -394,13 +388,12 @@
     return pl.pallas_call(
         main_kernel,
         out_shape=[jax.ShapeDtypeStruct((DEVS, 8, SEG), BF16)] * 2,
-        in_specs=[pl.BlockSpec(memory_space=pltpu.HBM)] + [vmem] * 4,
+        in_specs=[pl.BlockSpec(memory_space=pltpu.HBM), vmem],
         out_specs=[pl.BlockSpec(memory_space=pl.ANY)] * 2,
         scratch_shapes=[
             *[pltpu.VMEM((RING, 16, w), BF16) for w in WIDTHS],
             *[pltpu.VMEM((MEMBERS, 16, w), BF16) for w in WIDTHS],
             pltpu.VMEM((RING, 2, BINS), F32),
-            pltpu.VMEM((8, 128), jnp.int32),
             pltpu.VMEM((WIDE // 128, STATIONS, 256), BF16),
             pltpu.VMEM((BLOCKS, 8, 128), jnp.int32),
             pltpu.VMEM((BLOCKS, 2 * SHARE, STATIONS), BF16),
@@ -420,7 +413,7 @@
             dma((2,)), dma((2,)), dma((2,)), dma((RING,)),
         ],
         compiler_params=pltpu.CompilerParams(
-            collective_id=0, has_side_effects=True, vmem_limit_bytes=46 * 1024 * 1024
+            collective_id=0, has_side_effects=True, vmem_limit_bytes=52 * 1024 * 1024
         ),
     )(*operands)
 
@@ -435,13 +428,11 @@
     marks = jnp.maximum(marks, pltpu.roll(marks, rows - 1, 1))
     marks = jnp.maximum(marks, pltpu.roll(marks, rows - 2, 1))
     code = (marks.astype(jnp.int32) + place * PAIRS)[0:1]
-    parts = [[], []]
-    for k in range(SEGS):
-        want = lax.broadcasted_iota(jnp.int32, (PAIRS, rows), 0) + k * PAIRS
-        hot = jnp.where(want == code, F32(1), F32(0)).astype(BF16)
-        for p in range(0 if k < 3 else 1, 2):
-            parts[p].append(jnp.dot(hot, got[p], preferred_element_type=F32))
-    parts = parts[1] + parts[0]
+    want = lax.broadcasted_iota(jnp.int32, (SEGS * PAIRS, rows), 0)
+    hot = jnp.where(want == code, F32(1), F32(0)).astype(BF16)
+    near, far = [jnp.dot(hot, g, preferred_element_type=F32) for g in (got[1], got[0])]
+    parts = [near[k * PAIRS : (k + 1) * PAIRS] for k in range(SEGS)]
+    parts += [far[k * PAIRS : (k + 1) * PAIRS] for k in range(SEGS - 1)]
     sums = jnp.concatenate(parts, axis=1)
     even, odd = sums[:, :896], sums[:, SIDE : SIDE + 896]
     tiles = 7
@@ -475,9 +466,9 @@
 
 
 def local(spectra, stacks, pair_sta, pair_valid, owner, slot):
-    got_a, got_b = correlate_and_route(
-        spectra, pair_sta, pair_valid[None, :], owner.reshape(1, PAIRS), slot[None, :]
-    )
+    rows = [pair_sta, pair_valid[None, :], owner.reshape(1, PAIRS), slot[None, :]]
+    meta = jnp.pad(jnp.concatenate(rows, axis=0), ((0, 3), (0, 128 - PAIRS)))
+    got_a, got_b = correlate_and_route(spectra, meta)
     return add_rows(got_a, got_b, stacks)
 
 

time: 73 us -> 69.5 us (0.952)
  local copies, waits for them, and re-layouts: 3.92 us -> 0.01 us
  other arithmetic: 0 us -> 0.8 us
    unnamed x12 -> x2, local copies, waits for them, and re-layouts: 3.92 us -> 0.01 us
    concatenate x0 -> x1, other arithmetic: none -> 0.8 us  [local(): meta = jnp.pad(jnp.concatenate(rows, axis=0), ((0, 3), (0, 128 - PAIRS)))]
where the time goes in v5:
time: 69.5 us; the launch traced here: 69.4 us
  Pallas kernels  68.5 us (99%)
  other arithmetic  0.8 us (1%)
    pallas_call x1, Pallas kernels, correlate_and_route(): pl.pallas_call(main_kernel, out_shape=[jax.ShapeDtypeStruct((DEVS, 8, SEG...  66.5 us
    pallas_call x1, Pallas kernels, add_rows(): pl.pallas_call(stack_kernel, out_shape=jax.ShapeDtypeStruct(stacks.shape,...  2.06 us

profile of v5, /device:TPU:1, one launch (start us, length us, event | category | flops | bytes accessed | tf_op | source)
XLA Modules:
  0.0 69.4 jit_solution(1648208560481228255)
XLA Ops:
  0.0 0.0 copy-start
  0.0 0.8 %pad_add_fusion = s32[5,96]{1,0:T(8,128)S(1)} fusion(s32[1,96]{1,0:T(1,128)} %bitcast.3, s32[1,96]{1,0:T(1,128)} %bitcast.4, s32[1,96]{1,0:T(1,128)} %bitcast.5, s32[2,96]{1,0:T(2,128)} %param.8), kind=kLoop, calls=%fused_computation | loop fusion | flops 1440 | bytes 3840 | tf_op jit(solution)/shard_map/concatenate | solution.py:470
  0.8 66.5 %shard_map.64 = (bf16[128,8,256]{2,1,0:T(8,128)(2,1)S(1)}, bf16[128,8,256]{2,1,0:T(8,128)(2,1)S(1)}) custom-call(f32[8,2,18432]{2,1,0:T(2,128)} %spectra_ref.1, s32[8,128]{1,0:T(8,128)S(1)} %pad.4.meta_ref), custom_call_target="tpu_custom_call" | custom-call | tf_op jit(solution)/shard_map/pallas_call | solution.py:388
  67.3 0.0 copy-done
  67.3 2.1 %shard_map.65 = f32[96,1601]{1,0:T(8,128)} custom-call(bf16[128,8,256]{2,1,0:T(8,128)(2,1)S(1)} %get-tuple-element.7.got_a, bf16[128,8,256]{2,1,0:T(8,128)(2,1)S(1)} %get-tuple-element.8.got_b, f32[96,1601]{1,0:T(8,128)S(1)} %copy-done), custom_call_target="tpu_custom_call" | custom-call | tf_op jit(solution)/shard_map/pallas_call | solution.py:459
  (1 shorter events, 0.0 us)
Async XLA Ops:
  0.0 67.3 %copy-start = (f32[96,1601]{1,0:T(8,128)S(1)}, f32[96,1601]{1,0:T(8,128)}, u32[]{:S(2)}) copy-start(f32[96,1601]{1,0:T(8,128)} %stacks_ref.1) | copy-start | bytes 1844356

commit v6 on v5

--- a/solution.py
+++ b/solution.py
@@ -77,15 +77,19 @@
     barrier = pltpu.get_barrier_semaphore()
 
     def greet(i, carry):
-        peer = lax.rem(dev + i, DEVS)
         pl.semaphore_signal(
-            barrier, inc=1,
-            device_id={"grp": peer // MEMBERS, "sta": lax.rem(peer, MEMBERS)},
-            device_id_type=MESH,
+            barrier, inc=1, device_id={"grp": grp, "sta": lax.rem(me + i, MEMBERS)}, device_id_type=MESH
         )
         return carry
 
-    lax.fori_loop(1, DEVS, greet, 0)
+    def greet_across(i, carry):
+        pl.semaphore_signal(
+            barrier, inc=1, device_id={"grp": lax.rem(grp + i, GROUPS), "sta": me}, device_id_type=MESH
+        )
+        return carry
+
+    lax.fori_loop(1, GROUPS, greet_across, 0)
+    lax.fori_loop(1, MEMBERS, greet, 0)
 
     lane = lax.broadcasted_iota(jnp.int32, (128, 128), 1) // BAND
     sub = lax.broadcasted_iota(jnp.int32, (128, 128), 0) // BAND
@@ -113,7 +117,7 @@
         return carry
 
     lax.fori_loop(0, RING, whiten, 0)
-    pl.semaphore_wait(barrier, DEVS - 1)
+    pl.semaphore_wait(barrier, GROUPS - 1 + MEMBERS - 1)
 
     def send_ids(slot, peer):
         pltpu.make_async_remote_copy(

time: 69.5 us -> 67.5 us (0.971)
  Pallas kernels: 68.5 us -> 66.5 us
    pallas_call x1, Pallas kernels: 66.5 us -> 64.4 us  [correlate_and_route(): pl.pallas_call(main_kernel, out_shape=[jax.ShapeDtypeStruct((DEVS, 8, SEG...]
where the time goes in v6:
time: 67.5 us; the launch traced here: 67.3 us
  Pallas kernels  66.5 us (99%)
  other arithmetic  0.8 us (1%)
    pallas_call x1, Pallas kernels, correlate_and_route(): pl.pallas_call(main_kernel, out_shape=[jax.ShapeDtypeStruct((DEVS, 8, SEG...  64.4 us
    pallas_call x1, Pallas kernels, add_rows(): pl.pallas_call(stack_kernel, out_shape=jax.ShapeDtypeStruct(stacks.shape,...  2.06 us

profile of v6, /device:TPU:1, one launch (start us, length us, event | category | flops | bytes accessed | tf_op | source)
XLA Modules:
  0.0 67.3 jit_solution(7520613859424913726)
XLA Ops:
  0.0 0.0 copy-start
  0.0 0.8 %pad_add_fusion = s32[5,96]{1,0:T(8,128)S(1)} fusion(s32[1,96]{1,0:T(1,128)} %bitcast.3, s32[1,96]{1,0:T(1,128)} %bitcast.4, s32[1,96]{1,0:T(1,128)} %bitcast.5, s32[2,96]{1,0:T(2,128)} %param.8), kind=kLoop, calls=%fused_computation | loop fusion | flops 1440 | bytes 3840 | tf_op jit(solution)/shard_map/concatenate | solution.py:474
  0.8 64.4 %shard_map.64 = (bf16[128,8,256]{2,1,0:T(8,128)(2,1)S(1)}, bf16[128,8,256]{2,1,0:T(8,128)(2,1)S(1)}) custom-call(f32[8,2,18432]{2,1,0:T(2,128)} %spectra_ref.1, s32[8,128]{1,0:T(8,128)S(1)} %pad.4.meta_ref), custom_call_target="tpu_custom_call" | custom-call | tf_op jit(solution)/shard_map/pallas_call | solution.py:392
  65.3 0.0 copy-done
  65.3 2.1 %shard_map.65 = f32[96,1601]{1,0:T(8,128)} custom-call(bf16[128,8,256]{2,1,0:T(8,128)(2,1)S(1)} %get-tuple-element.7.got_a, bf16[128,8,256]{2,1,0:T(8,128)(2,1)S(1)} %get-tuple-element.8.got_b, f32[96,1601]{1,0:T(8,128)S(1)} %copy-done), custom_call_target="tpu_custom_call" | custom-call | tf_op jit(solution)/shard_map/pallas_call | solution.py:463
  (1 shorter events, 0.0 us)
Async XLA Ops:
  0.0 65.3 %copy-start = (f32[96,1601]{1,0:T(8,128)S(1)}, f32[96,1601]{1,0:T(8,128)}, u32[]{:S(2)}) copy-start(f32[96,1601]{1,0:T(8,128)} %stacks_ref.1) | copy-start | bytes 1844356

commit v7 on v6

--- a/solution.py
+++ b/solution.py
@@ -358,17 +358,22 @@
         own.start()
         owns.append(own)
 
+        def send_row(there, member):
+            pltpu.make_async_remote_copy(
+                src_ref=c_send[p].at[there * MEMBERS + member], dst_ref=got[p].at[dev],
+                send_sem=c_send_sem.at[p], recv_sem=c_recv_sem.at[p],
+                device_id={"grp": there, "sta": member}, device_id_type=MESH,
+            ).start()
+
         def route(i, carry):
-            peer = lax.rem(dev + i * 53, DEVS)
-            pltpu.make_async_remote_copy(
-                src_ref=c_send[p].at[peer], dst_ref=got[p].at[dev],
-                send_sem=c_send_sem.at[p], recv_sem=c_recv_sem.at[p],
-                device_id={"grp": peer // MEMBERS, "sta": lax.rem(peer, MEMBERS)},
-                device_id_type=MESH,
-            ).start()
+            member = lax.rem(me + i * 11, MEMBERS)
+            for g in (2, 1, 3, 0):
+                send_row(lax.rem(grp + g, GROUPS), member)
             return carry
 
-        lax.fori_loop(1, DEVS, route, 0)
+        for g in (2, 1, 3):
+            send_row(lax.rem(grp + g, GROUPS), me)
+        lax.fori_loop(1, MEMBERS, route, 0)
 
     for p in range(2):
         for copy in a_copies[p]:

time: 67.5 us -> 67.5 us (level)
  no operation moved by 1% of the time
where the time goes in v7:
time: 67.5 us; the launch traced here: 67.4 us
  Pallas kernels  66.6 us (99%)
  other arithmetic  0.8 us (1%)
    pallas_call x1, Pallas kernels, correlate_and_route(): pl.pallas_call(main_kernel, out_shape=[jax.ShapeDtypeStruct((DEVS, 8, SEG...  64.5 us
    pallas_call x1, Pallas kernels, add_rows(): pl.pallas_call(stack_kernel, out_shape=jax.ShapeDtypeStruct(stacks.shape,...  2.06 us

profile of v7, /device:TPU:1, one launch (start us, length us, event | category | flops | bytes accessed | tf_op | source)
XLA Modules:
  0.0 67.4 jit_solution(18030605181173458503)
XLA Ops:
  0.0 0.0 copy-start
  0.0 0.8 %pad_add_fusion = s32[5,96]{1,0:T(8,128)S(1)} fusion(s32[1,96]{1,0:T(1,128)} %bitcast.3, s32[1,96]{1,0:T(1,128)} %bitcast.4, s32[1,96]{1,0:T(1,128)} %bitcast.5, s32[2,96]{1,0:T(2,128)} %param.8), kind=kLoop, calls=%fused_computation | loop fusion | flops 1440 | bytes 3840 | tf_op jit(solution)/shard_map/concatenate | solution.py:479
  0.8 64.5 %shard_map.64 = (bf16[128,8,256]{2,1,0:T(8,128)(2,1)S(1)}, bf16[128,8,256]{2,1,0:T(8,128)(2,1)S(1)}) custom-call(f32[8,2,18432]{2,1,0:T(2,128)} %spectra_ref.1, s32[8,128]{1,0:T(8,128)S(1)} %pad.4.meta_ref), custom_call_target="tpu_custom_call" | custom-call | tf_op jit(solution)/shard_map/pallas_call | solution.py:397
  65.3 0.0 copy-done
  65.4 2.1 %shard_map.65 = f32[96,1601]{1,0:T(8,128)} custom-call(bf16[128,8,256]{2,1,0:T(8,128)(2,1)S(1)} %get-tuple-element.7.got_a, bf16[128,8,256]{2,1,0:T(8,128)(2,1)S(1)} %get-tuple-element.8.got_b, f32[96,1601]{1,0:T(8,128)S(1)} %copy-done), custom_call_target="tpu_custom_call" | custom-call | tf_op jit(solution)/shard_map/pallas_call | solution.py:468
  (1 shorter events, 0.0 us)
Async XLA Ops:
  0.0 65.3 %copy-start = (f32[96,1601]{1,0:T(8,128)S(1)}, f32[96,1601]{1,0:T(8,128)}, u32[]{:S(2)}) copy-start(f32[96,1601]{1,0:T(8,128)} %stacks_ref.1) | copy-start | bytes 1844356
